TPU v7x, 256 devices: a whole 4x4x8 slice. The times are simulated.
256 devices in a mesh: ctx: 64 (over z, x_hi, y), chan: 4 (over x_lo, core).
Axes of the slice: x: 4 (x_hi: 2, x_lo: 2; x = x_hi * 2 + x_lo), y: 4, z: 8, core: 2. Of those that a mesh axis runs over, the one named last changes fastest.
Arguments:
- projected: bfloat16 [16384, 3, 4096], P('ctx', None, 'chan'), may hold values from -6 to 6
- short_taps: float32 [3, 3, 4096], P(None, None, 'chan'), may hold values from -3 to 3
- decay_rates: float32 [4096, 16], P('chan'), may hold values from 0 to 0.034, as said below
- residues: float32 [4096, 16], P('chan')
- out_weight: bfloat16 [4096, 4096], P(None, 'chan'), may hold values from -0.09375 to 0.09375
Outputs:
- mixed: bfloat16 [16384, 4096], P('ctx', 'chan')
Inputs may be any that keep to these rules, and one draw needn't show every extreme that they name: `decay_rates`: every decay rate is positive.
All inputs are finite; a program needn't handle non-finite values.
Results may differ from a plain program's by a relative error of at most 0.0049.
Values may be sent and summed in bfloat16 or wider, within the bound.
No kernel may reach another device: no remote copies, remote signals or barrier semaphores. Data moves between devices by JAX's collectives and lax.ppermute only.
A program may use at most 128 MiB of HBM per device.

v0:
```python
import functools

import jax
import jax.numpy as jnp
from jax import lax
from jax.experimental import pallas as pl
from jax.experimental.pallas import tpu as pltpu
from jax.sharding import PartitionSpec as P

TAPS = 3
LANES = 128
ROWS = 8
CHUNKS = 4
VMEM = pl.BlockSpec(memory_space=pltpu.VMEM)


def params(mib):
    return pltpu.CompilerParams(vmem_limit_bytes=mib * 1024 * 1024)


def short_filter(x_ref, first, taps, lanes):
    block = x_ref.shape[0] - ROWS
    out = taps[0:1, lanes] * x_ref[pl.ds(ROWS, block), :]
    out = out + taps[1:2, lanes] * x_ref[pl.ds(ROWS - 1, block), :]
    return out + taps[2:3, lanes] * x_ref[pl.ds(ROWS - 2, block), :]


def end_state_kernel(p_ref, taps_ref, rates_ref, out_ref, k_ref, v_ref, u_ref):
    block, channels = p_ref.shape[1:]
    k_ref[pl.ds(0, ROWS), :] = jnp.zeros((ROWS, LANES), jnp.float32)
    v_ref[pl.ds(0, ROWS), :] = jnp.zeros((ROWS, LANES), jnp.float32)
    modes = rates_ref.shape[0]
    row = lax.broadcasted_iota(jnp.int32, (ROWS, LANES), 0).astype(jnp.float32)

    def lane_block(c, carry):
        lanes = pl.ds(pl.multiple_of(c * LANES, LANES), LANES)
        k_ref[pl.ds(ROWS, block), :] = p_ref[1, :, lanes].astype(jnp.float32)
        v_ref[pl.ds(ROWS, block), :] = p_ref[2, :, lanes].astype(jnp.float32)
        u = short_filter(k_ref, 0, taps_ref.at[1], lanes) * short_filter(v_ref, 0, taps_ref.at[2], lanes)
        u_ref[...] = u
        u_ref[pl.ds(0, ROWS), :] = jnp.where(row < TAPS - 1, 0.0, u[:ROWS])
        rates = [jnp.broadcast_to(rates_ref[m : m + 1, lanes], (ROWS, LANES)) for m in range(modes)]
        steps = [jnp.exp(-float(ROWS) * r) for r in rates]
        state = [u_ref[pl.ds(0, ROWS), :]] * modes
        for j in range(1, block // ROWS):
            now = u_ref[pl.ds(j * ROWS, ROWS), :]
            state = [a * s + now for a, s in zip(steps, state)]
        for m in range(modes):
            weighted = state[m] * jnp.exp(rates[m] * (row - (ROWS - 1.0)))
            out_ref[m : m + 1, lanes] = jnp.sum(weighted, axis=0, keepdims=True)
        return carry

    lax.fori_loop(0, channels // LANES, lane_block, 0)


def end_state(p, taps, rates):
    block, channels = p.shape[1:]
    return pl.pallas_call(
        end_state_kernel,
        out_shape=jax.ShapeDtypeStruct(rates.shape, jnp.float32),
        in_specs=[VMEM] * 3,
        out_specs=VMEM,
        scratch_shapes=[
            pltpu.VMEM((ROWS + block, LANES), jnp.float32),
            pltpu.VMEM((ROWS + block, LANES), jnp.float32),
            pltpu.VMEM((block, LANES), jnp.float32),
        ],
        compiler_params=params(16),
        name="end_state",
    )(p, taps, rates)


def local_kernel(p_ref, prev_ref, taps_ref, rates_ref, res_ref, y_ref, q_out_ref, x_ref, u_ref, a_ref, r_ref):
    block, channels = p_ref.shape[1:]
    modes = rates_ref.shape[0]
    groups, cblocks = block // ROWS, channels // LANES
    for c in range(cblocks):
        lanes = pl.ds(c * LANES, LANES)
        feats = []
        for i in range(3):
            before = prev_ref[i, :, lanes].astype(jnp.float32)
            x_ref[pl.ds(ROWS - 2, 2), :] = before
            x_ref[pl.ds(ROWS, block), :] = p_ref[i, :, lanes].astype(jnp.float32)
            feats.append(short_filter(x_ref, 0, taps_ref.at[i], lanes))
        u = feats[1] * feats[2]
        for j in range(groups):
            rows = pl.ds(j * ROWS * cblocks + c * ROWS, ROWS)
            u_ref[rows, :] = u[j * ROWS : (j + 1) * ROWS]
            q_out_ref[rows, :] = feats[0][j * ROWS : (j + 1) * ROWS]
        for m in range(0, modes, ROWS):
            rows = pl.ds(m * cblocks + c, ROWS, stride=cblocks)
            a_ref[rows, :] = jnp.exp(-rates_ref[m : m + ROWS, lanes])
            r_ref[rows, :] = res_ref[m : m + ROWS, lanes]

    def group(j, state):
        state = list(state)
        for i in range(ROWS):
            at = pl.ds(j * ROWS * cblocks + i, cblocks, stride=ROWS)
            now = u_ref[at, :]
            total = [None] * 4
            for m in range(modes):
                a = a_ref[pl.ds(m * cblocks, cblocks), :]
                r = r_ref[pl.ds(m * cblocks, cblocks), :]
                state[m] = a * state[m] + now
                term = r * state[m]
                total[m % 4] = term if total[m % 4] is None else total[m % 4] + term
            y_ref[at, :] = (total[0] + total[1]) + (total[2] + total[3])
        return tuple(state)

    zero = jnp.zeros((cblocks, LANES), jnp.float32)
    lax.fori_loop(0, groups, group, (zero,) * modes)


def local_part(p, prev, taps, rates, residues):
    block, channels = p.shape[1:]
    modes = rates.shape[0]
    cblocks = channels // LANES
    tiled = jax.ShapeDtypeStruct((block * cblocks, LANES), jnp.float32)
    return pl.pallas_call(
        local_kernel,
        out_shape=(tiled, tiled),
        in_specs=[VMEM] * 5,
        out_specs=(VMEM, VMEM),
        scratch_shapes=[
            pltpu.VMEM((ROWS + block, LANES), jnp.float32),
            pltpu.VMEM((block * cblocks, LANES), jnp.float32),
            pltpu.VMEM((modes * cblocks, LANES), jnp.float32),
            pltpu.VMEM((modes * cblocks, LANES), jnp.float32),
        ],
        compiler_params=params(16),
        cost_estimate=pl.CostEstimate(flops=4 * modes * block * channels, bytes_accessed=6 * block * channels, transcendentals=0),
        name="local_part",
    )(p, prev, taps, rates, residues)


def gate_kernel(y_ref, q_ref, state_ref, rates_ref, res_ref, out_ref):
    groups, cblocks = y_ref.shape[:2]
    modes = rates_ref.shape[0]
    row = lax.broadcasted_iota(jnp.int32, (ROWS, LANES), 0).astype(jnp.float32)
    for c in range(cblocks):
        lanes = pl.ds(c * LANES, LANES)
        terms, steps = [], []
        for m in range(modes):
            rate = jnp.broadcast_to(rates_ref[m : m + 1, lanes], (ROWS, LANES))
            scale = res_ref[m : m + 1, lanes] * state_ref[m : m + 1, lanes]
            terms.append(jnp.exp(-rate * (row + 1.0)) * scale)
            steps.append(jnp.exp(-float(ROWS) * rate))

        def pair(jj, terms):
            terms = list(terms)
            halves = []
            for half in range(2):
                total = [y_ref[2 * jj + half, c], None, None, None]
                for m in range(modes):
                    total[m % 4] = terms[m] if total[m % 4] is None else total[m % 4] + terms[m]
                    terms[m] = terms[m] * steps[m]
                halves.append(q_ref[2 * jj + half, c] * ((total[0] + total[1]) + (total[2] + total[3])))
            both = jnp.concatenate(halves, axis=0).astype(out_ref.dtype)
            out_ref[pl.ds(pl.multiple_of(jj * 2 * ROWS, 2 * ROWS), 2 * ROWS), lanes] = both
            return tuple(terms)

        lax.fori_loop(0, groups // 2, pair, tuple(terms), unroll=4)


def gate(part, parts, y, q, state, rates, residues):
    modes, channels = rates.shape
    cblocks = channels // LANES
    block = y.shape[0] // cblocks
    y, q = (value.reshape(block // ROWS, cblocks, ROWS, LANES) for value in (y, q))
    own = cblocks // parts
    rows = pl.BlockSpec((block // ROWS, own, ROWS, LANES), lambda g: (0, part, 0, 0))
    table = pl.BlockSpec((modes, own * LANES), lambda g: (0, part))
    return pl.pallas_call(
        gate_kernel,
        grid=(1,),
        out_shape=jax.ShapeDtypeStruct((block, own * LANES), jnp.bfloat16),
        in_specs=[rows, rows, table, table, table],
        out_specs=pl.BlockSpec((block, own * LANES), lambda g: (0, 0)),
        compiler_params=params(16),
        cost_estimate=pl.CostEstimate(flops=2 * modes * block * own * LANES, bytes_accessed=10 * block * own * LANES, transcendentals=0),
        name="gate",
    )(y, q, state, rates, residues)


def project_kernel(last, order_ref, acc_ref, p0, p1, p2, p3, w_ref, out_ref, total_ref):
    step = pl.program_id(0)

    @pl.when(step == 0)
    def _():
        total_ref[...] = acc_ref[...] if acc_ref is not None else jnp.zeros_like(total_ref)

    for number, piece in enumerate((p0, p1, p2, p3)):

        @pl.when(step == number)
        def _():
            total_ref[...] += jnp.dot(piece[...], w_ref[...], preferred_element_type=jnp.float32)

    @pl.when(step == 3)
    def _():
        out_ref[...] = total_ref[...].astype(out_ref.dtype)


def project(part, parts, order, acc, pieces, weight):
    block, depth = pieces[0].shape
    features = weight.shape[1]
    last = part == parts - 1
    whole = lambda shape: pl.BlockSpec(shape, lambda g, order: (0, 0))
    kernel = functools.partial(project_kernel, last)
    if acc is None:
        kernel = lambda order_ref, *refs: project_kernel(last, order_ref, None, *refs)
    grid_spec = pltpu.PrefetchScalarGridSpec(
        num_scalar_prefetch=1,
        grid=(4,),
        in_specs=([] if acc is None else [whole((block, features))])
        + [whole((block, depth))] * 4
        + [pl.BlockSpec((depth, features), lambda g, order: (order[g] * parts + part, 0))],
        out_specs=whole((block, features)),
        scratch_shapes=[pltpu.VMEM((block, features), jnp.float32)],
    )
    return pl.pallas_call(
        kernel,
        grid_spec=grid_spec,
        out_shape=jax.ShapeDtypeStruct((block, features), jnp.bfloat16 if last else jnp.float32),
        compiler_params=params(16),
        cost_estimate=pl.CostEstimate(flops=8 * block * depth * features, bytes_accessed=8 * depth * features, transcendentals=0),
        name="project",
    )(order, *(() if acc is None else (acc,)), *pieces, weight)


def partners(count):
    levels, size = [], 1
    while size < count:
        if size in (2, 32):
            ring = 4 if size == 2 else 8
            unit = size * 2 // ring
            flip = lambda i: (i // (unit * ring)) * unit * ring + (ring - 1 - i // unit % ring) * unit + i % unit
        else:
            flip = lambda i: i ^ size
        levels.append((size, [flip(i) for i in range(count)]))
        size *= 2
    return levels


def states_before(end, rates, block):
    count = lax.axis_size("ctx")
    position = lax.axis_index("ctx")
    total, before = end, jnp.zeros_like(end)
    for size, partner in partners(count):
        other = lax.ppermute(total, "ctx", list(enumerate(partner)))
        later = (position // size) % 2 == 1
        offset = (position % size).astype(jnp.float32)
        decay = jnp.exp(-rates * (block * offset))
        before = before + jnp.where(later, other * decay, 0.0)
        whole = jnp.exp(-rates * float(block * size))
        total = jnp.where(later, other * whole + total, total * whole + other)
    return before


def per_device(projected, short_taps, decay_rates, residues, out_weight):
    block = projected.shape[0]
    count = lax.axis_size("ctx")
    p = projected.transpose(1, 0, 2)
    rates, res = decay_rates.T, residues.T

    prev = lax.ppermute(p[:, block - (TAPS - 1) :], "ctx", [(i, i + 1) for i in range(count - 1)])
    end = end_state(p, short_taps, rates)
    head = jnp.concatenate([prev, p[:, : TAPS - 1]], axis=1).astype(jnp.float32)
    feats = sum(short_taps[:, j, None] * head[:, TAPS - 1 - j : 2 * (TAPS - 1) - j] for j in range(TAPS))
    first = feats[1] * feats[2]
    for t in range(TAPS - 1):
        end = end + jnp.exp(-rates * float(block - 1 - t)) * first[t][None]

    before = states_before(end, rates, block)
    y, q = local_part(p, prev, short_taps, rates, res)

    own = lax.axis_index("chan")
    order = jnp.stack([own, own ^ 2, own ^ 1, own ^ 3]).astype(jnp.int32)
    over_x = [(i, i ^ 2) for i in range(4)]
    over_core = [(i, i ^ 1) for i in range(4)]
    acc = None
    for part in range(CHUNKS):
        mine = gate(part, CHUNKS, y, q, before, rates, res)
        across = lax.ppermute(mine, "chan", over_x)
        beside = lax.ppermute(mine, "chan", over_core)
        far = lax.ppermute(across, "chan", over_core)
        acc = project(part, CHUNKS, order, acc, (mine, across, beside, far), out_weight)
    return acc


def solution(mesh):
    in_specs = (
        P("ctx", None, "chan"),
        P(None, None, "chan"),
        P("chan", None),
        P("chan", None),
        P(None, "chan"),
    )
    return jax.shard_map(
        per_device, mesh=mesh, in_specs=in_specs, out_specs=P("ctx", "chan"), check_vma=False
    )
```

profile of v0, /device:TPU:1, one launch (start us, length us, event | category | flops | bytes accessed | tf_op | source)
XLA Modules:
  0.0 77.7 jit_solution(15425339657794977233)
XLA Ops:
  0.0 0.0 copy-start.3
  0.0 0.9 %fusion.2 = (bf16[3,2,1024]{2,1,0:T(2,128)(2,1)S(1)}, bf16[3,2,1024]{2,1,0:T(2,128)(2,1)S(1)}) fusion(bf16[3,256,1024]{2,1,0:T(8,128)(2,1)} %bitcast.39), kind=kLoop, calls=%fused_computation.18 | loop fusion | bytes 49152 | tf_op jit(solution)/shard_map/slice | solution.py:267
  0.9 4.0 %collective-permute-start = (bf16[3,2,1024]{2,1,0:T(2,128)(2,1)S(1)}, bf16[3,2,1024]{2,1,0:T(2,128)(2,1)S(1)}, u32[]{:S(2)}, u32[]{:S(2)}) collective-permute-start(bf16[3,2,1024]{2,1,0:T(2,128)(2,1)S(1)} %get-tuple-element.10), channel_id=1, source_target_pairs={{0,4},{4,8},{8,12},{12,16},{16,20},{20,24},{24,28},{28,32},{32,36}... | collective-permute-start | bytes 36872 | tf_op jit(solution)/shard_map/ppermute | solution.py:265
  4.9 0.9 %fusion.3 = (f32[3,1,1024]{2,1,0:T(1,128)S(1)}, f32[3,1,1024]{2,1,0:T(1,128)S(1)}, f32[3,1,1024]{2,1,0:T(1,128)S(1)}) fusion(f32[3,3,1024]{2,1,0:T(4,128)} %taps_ref.3), kind=kLoop, calls=%fused_computation.19 | loop fusion | bytes 73728 | tf_op jit(solution)/shard_map/slice | solution.py:268
  5.9 0.0 copy-start.2
  5.9 0.8 %copy-done.2 = f32[1024,16]{0,1:T(8,128)S(1)} copy-done((f32[1024,16]{0,1:T(8,128)S(1)}, f32[1024,16]{0,1:T(8,128)}, u32[]{:S(2)}) %copy-start.2) | copy-done | bytes 65560
  6.7 0.0 copy-start.4
  6.8 1.4 %copy-done.4 = bf16[256,3,1024]{2,0,1:T(8,128)(2,1)S(1)} copy-done((bf16[256,3,1024]{2,0,1:T(8,128)(2,1)S(1)}, bf16[256,3,1024]{2,0,1:T(8,128)(2,1)}, u32[]{:S(2)}) %copy-start.4) | copy-done | bytes 1572888
  8.2 0.8 %copy-done.7 = f32[3,3,1024]{2,1,0:T(4,128)S(1)} copy-done((f32[3,3,1024]{2,1,0:T(4,128)S(1)}, f32[3,3,1024]{2,1,0:T(4,128)}, u32[]{:S(2)}) %copy-start.7) | copy-done | bytes 36888
  9.0 2.2 %end_state.1 = f32[16,1024]{1,0:T(8,128)S(1)} custom-call(bf16[3,256,1024]{2,1,0:T(8,128)(2,1)S(1)} %bitcast.40, f32[3,3,1024]{2,1,0:T(4,128)S(1)} %copy-done.7, f32[16,1024]{1,0:T(8,128)S(1)} %bitcast.33), custom_call_target="tpu_custom_call" | custom-call | tf_op jit(solution)/shard_map/end_state/pallas_call | solution.py:58
  11.2 0.0 collective-permute-done.prev_ref
  11.3 1.4 %collective-permute-start.1 = (f32[16,1024]{1,0:T(8,128)S(1)}, f32[16,1024]{1,0:T(8,128)S(1)}, u32[]{:S(2)}, u32[]{:S(2)}) collective-permute-start(f32[16,1024]{1,0:T(8,128)S(1)} %multiply_add_fusion), channel_id=1, source_target_pairs={{0,4},{4,0},{8,12},{12,8},{16,20},{20,16},{24,28},{28,24},{32,36},... | collective-permute-start | bytes 196616 | tf_op jit(solution)/shard_map/ppermute | solution.py:249
  12.7 1.8 %collective-permute-done.1 = f32[16,1024]{1,0:T(8,128)S(1)} collective-permute-done((f32[16,1024]{1,0:T(8,128)S(1)}, f32[16,1024]{1,0:T(8,128)S(1)}, u32[]{:S(2)}, u32[]{:S(2)}) %collective-permute-start.1) | collective-permute-done | bytes 65568 | tf_op jit(solution)/shard_map/ppermute | solution.py:249
  14.5 0.0 copy-done.3
  14.6 3.9 %collective-permute-start.2 = (f32[16,1024]{1,0:T(8,128)S(1)}, f32[16,1024]{1,0:T(8,128)S(1)}, u32[]{:S(2)}, u32[]{:S(2)}) collective-permute-start(f32[16,1024]{1,0:T(8,128)S(1)} %add_select_fusion.4), channel_id=1, source_target_pairs={{0,12},{4,8},{8,4},{12,0},{16,28},{20,24},{24,20},{28,16},{32,44},... | collective-permute-start | bytes 196616 | tf_op jit(solution)/shard_map/ppermute | solution.py:249
  18.5 1.7 %collective-permute-done.2 = f32[16,1024]{1,0:T(8,128)S(1)} collective-permute-done((f32[16,1024]{1,0:T(8,128)S(1)}, f32[16,1024]{1,0:T(8,128)S(1)}, u32[]{:S(2)}, u32[]{:S(2)}) %collective-permute-start.2) | collective-permute-done | bytes 65568 | tf_op jit(solution)/shard_map/ppermute | solution.py:249
  20.2 1.7 %collective-permute-start.3 = (f32[16,1024]{1,0:T(8,128)S(1)}, f32[16,1024]{1,0:T(8,128)S(1)}, u32[]{:S(2)}, u32[]{:S(2)}) collective-permute-start(f32[16,1024]{1,0:T(8,128)S(1)} %add_select_fusion.3), channel_id=1, source_target_pairs={{0,16},{4,20},{8,24},{12,28},{16,0},{20,4},{24,8},{28,12},{32,48},... | collective-permute-start | bytes 196616 | tf_op jit(solution)/shard_map/ppermute | solution.py:249
  21.8 3.0 %collective-permute-done.3 = f32[16,1024]{1,0:T(8,128)S(1)} collective-permute-done((f32[16,1024]{1,0:T(8,128)S(1)}, f32[16,1024]{1,0:T(8,128)S(1)}, u32[]{:S(2)}, u32[]{:S(2)}) %collective-permute-start.3) | collective-permute-done | bytes 65568 | tf_op jit(solution)/shard_map/ppermute | solution.py:249
  24.9 1.7 %collective-permute-start.4 = (f32[16,1024]{1,0:T(8,128)S(1)}, f32[16,1024]{1,0:T(8,128)S(1)}, u32[]{:S(2)}, u32[]{:S(2)}) collective-permute-start(f32[16,1024]{1,0:T(8,128)S(1)} %add_select_fusion.2), channel_id=1, source_target_pairs={{0,32},{4,36},{8,40},{12,44},{16,48},{20,52},{24,56},{28,60},{32,0... | collective-permute-start | bytes 196616 | tf_op jit(solution)/shard_map/ppermute | solution.py:249
  26.6 2.0 %collective-permute-done.4 = f32[16,1024]{1,0:T(8,128)S(1)} collective-permute-done((f32[16,1024]{1,0:T(8,128)S(1)}, f32[16,1024]{1,0:T(8,128)S(1)}, u32[]{:S(2)}, u32[]{:S(2)}) %collective-permute-start.4) | collective-permute-done | bytes 65568 | tf_op jit(solution)/shard_map/ppermute | solution.py:249
  28.6 3.1 %collective-permute-start.5 = (f32[16,1024]{1,0:T(8,128)S(1)}, f32[16,1024]{1,0:T(8,128)S(1)}, u32[]{:S(2)}, u32[]{:S(2)}) collective-permute-start(f32[16,1024]{1,0:T(8,128)S(1)} %add_select_fusion.1), channel_id=1, source_target_pairs={{0,64},{4,68},{8,72},{12,76},{16,80},{20,84},{24,88},{28,92},{32,9... | collective-permute-start | bytes 196616 | tf_op jit(solution)/shard_map/ppermute | solution.py:249
  31.7 1.7 %collective-permute-done.5 = f32[16,1024]{1,0:T(8,128)S(1)} collective-permute-done((f32[16,1024]{1,0:T(8,128)S(1)}, f32[16,1024]{1,0:T(8,128)S(1)}, u32[]{:S(2)}, u32[]{:S(2)}) %collective-permute-start.5) | collective-permute-done | bytes 65568 | tf_op jit(solution)/shard_map/ppermute | solution.py:249
  33.4 5.5 %collective-permute-start.6 = (f32[16,1024]{1,0:T(8,128)S(1)}, f32[16,1024]{1,0:T(8,128)S(1)}, u32[]{:S(2)}, u32[]{:S(2)}) collective-permute-start(f32[16,1024]{1,0:T(8,128)S(1)} %add_select_fusion), channel_id=1, source_target_pairs={{0,224},{4,228},{8,232},{12,236},{16,240},{20,244},{24,248},{28,25... | collective-permute-start | bytes 196616 | tf_op jit(solution)/shard_map/ppermute | solution.py:249
  38.9 0.0 copy-done.5
  38.9 0.0 copy-done.6
  38.9 0.0 copy-done.8
  38.9 3.7 %local_part.1 = (f32[2048,128]{1,0:T(8,128)S(1)}, f32[2048,128]{1,0:T(8,128)S(1)}) custom-call(bf16[3,256,1024]{2,1,0:T(8,128)(2,1)S(1)} %bitcast.41, bf16[3,2,1024]{2,1,0:T(2,128)(2,1)S(1)} %collective-permute-done.prev_ref, f32[3,3,1024]{2,1,0:T(4,128)S(1)} %copy-done.8, f32[16,1024]{1,0:T(8,128)S(1)} %bitcast.34, f32[16,1024]{1,0:T(8,128)S(1)} %bitcast.42), custom_call_target="tpu_custom_call" | custom-call | flops 16777216 | bytes 1572864 | tf_op jit(solution)/shard_map/local_part/pallas_call | solution.py:119
  42.6 0.0 collective-permute-done.6
  42.6 0.1 select_add_fusion.state_ref
  42.7 0.4 gate.4.refs_0_
  43.2 6.9 %collective-permute-start.8 = (bf16[256,256]{1,0:T(8,128)(2,1)S(1)}, bf16[256,256]{1,0:T(8,128)(2,1)S(1)}, u32[]{:S(2)}, u32[]{:S(2)}) collective-permute-start(bf16[256,256]{1,0:T(8,128)(2,1)S(1)} %gate.4.refs_0_), channel_id=1, source_target_pairs={{0,1},{1,0},{2,3},{3,2},{4,5},{5,4},{6,7},{7,6},{8,9},{9,8},{10,11... | collective-permute-start | bytes 393224 | tf_op jit(solution)/shard_map/ppermute | solution.py:284
  50.1 0.3 collective-permute-start.7
  50.4 0.4 gate.5.p0
  50.9 0.4 collective-permute-start.11
  51.3 1.2 %collective-permute-start.10 = (bf16[256,256]{1,0:T(8,128)(2,1)S(1)}, bf16[256,256]{1,0:T(8,128)(2,1)S(1)}, u32[]{:S(2)}, u32[]{:S(2)}) collective-permute-start(bf16[256,256]{1,0:T(8,128)(2,1)S(1)} %gate.5.p0), channel_id=1, source_target_pairs={{0,2},{1,3},{2,0},{3,1},{4,6},{5,7},{6,4},{7,5},{8,10},{9,11},{10,... | collective-permute-start | bytes 393224 | tf_op jit(solution)/shard_map/ppermute | solution.py:283
  52.5 0.4 gate.6.p0
  52.9 0.4 collective-permute-start.13
  53.3 0.4 gate.7.p0
  53.7 0.0 collective-permute-done.8.refs_2_
  53.7 1.3 %collective-permute-start.16 = (bf16[256,256]{1,0:T(8,128)(2,1)S(1)}, bf16[256,256]{1,0:T(8,128)(2,1)S(1)}, u32[]{:S(2)}, u32[]{:S(2)}) collective-permute-start(bf16[256,256]{1,0:T(8,128)(2,1)S(1)} %gate.7.p0), channel_id=1, source_target_pairs={{0,2},{1,3},{2,0},{3,1},{4,6},{5,7},{6,4},{7,5},{8,10},{9,11},{10,... | collective-permute-start | bytes 393224 | tf_op jit(solution)/shard_map/ppermute | solution.py:283
  55.0 0.2 collective-permute-done.7.refs_1_
  55.2 1.3 %collective-permute-start.9 = (bf16[256,256]{1,0:T(8,128)(2,1)S(1)}, bf16[256,256]{1,0:T(8,128)(2,1)S(1)}, u32[]{:S(2)}, u32[]{:S(2)}) collective-permute-start(bf16[256,256]{1,0:T(8,128)(2,1)S(1)} %collective-permute-done.7.refs_1_), channel_id=1, source_target_pairs={{0,1},{1,0},{2,3},{3,2},{4,5},{5,4},{6,7},{7,6},{8,9},{9,8},{10,11... | collective-permute-start | bytes 393224 | tf_op jit(solution)/shard_map/ppermute | solution.py:285
  56.5 0.0 collective-permute-done.11.p2
  56.5 0.0 collective-permute-start.14
  56.5 1.5 %collective-permute-done.10.p1 = bf16[256,256]{1,0:T(8,128)(2,1)S(1)} collective-permute-done((bf16[256,256]{1,0:T(8,128)(2,1)S(1)}, bf16[256,256]{1,0:T(8,128)(2,1)S(1)}, u32[]{:S(2)}, u32[]{:S(2)}) %collective-permute-start.10) | collective-permute-done | bytes 131104 | tf_op jit(solution)/shard_map/ppermute | solution.py:283
  58.0 1.3 %collective-permute-start.12 = (bf16[256,256]{1,0:T(8,128)(2,1)S(1)}, bf16[256,256]{1,0:T(8,128)(2,1)S(1)}, u32[]{:S(2)}, u32[]{:S(2)}) collective-permute-start(bf16[256,256]{1,0:T(8,128)(2,1)S(1)} %collective-permute-done.10.p1), channel_id=1, source_target_pairs={{0,1},{1,0},{2,3},{3,2},{4,5},{5,4},{6,7},{7,6},{8,9},{9,8},{10,11... | collective-permute-start | bytes 393224 | tf_op jit(solution)/shard_map/ppermute | solution.py:285
  59.3 1.5 %collective-permute-done.13.p1 = bf16[256,256]{1,0:T(8,128)(2,1)S(1)} collective-permute-done((bf16[256,256]{1,0:T(8,128)(2,1)S(1)}, bf16[256,256]{1,0:T(8,128)(2,1)S(1)}, u32[]{:S(2)}, u32[]{:S(2)}) %collective-permute-start.13) | collective-permute-done | bytes 131104 | tf_op jit(solution)/shard_map/ppermute | solution.py:283
  60.8 1.3 %collective-permute-start.15 = (bf16[256,256]{1,0:T(8,128)(2,1)S(1)}, bf16[256,256]{1,0:T(8,128)(2,1)S(1)}, u32[]{:S(2)}, u32[]{:S(2)}) collective-permute-start(bf16[256,256]{1,0:T(8,128)(2,1)S(1)} %collective-permute-done.13.p1), channel_id=1, source_target_pairs={{0,1},{1,0},{2,3},{3,2},{4,5},{5,4},{6,7},{7,6},{8,9},{9,8},{10,11... | collective-permute-start | bytes 393224 | tf_op jit(solution)/shard_map/ppermute | solution.py:285
  62.1 0.1 pad_add_fusion.order_ref
  62.2 1.4 %collective-permute-done.16.p1 = bf16[256,256]{1,0:T(8,128)(2,1)S(1)} collective-permute-done((bf16[256,256]{1,0:T(8,128)(2,1)S(1)}, bf16[256,256]{1,0:T(8,128)(2,1)S(1)}, u32[]{:S(2)}, u32[]{:S(2)}) %collective-permute-start.16) | collective-permute-done | bytes 131104 | tf_op jit(solution)/shard_map/ppermute | solution.py:283
  63.6 0.9 %collective-permute-start.17 = (bf16[256,256]{1,0:T(8,128)(2,1)S(1)}, bf16[256,256]{1,0:T(8,128)(2,1)S(1)}, u32[]{:S(2)}, u32[]{:S(2)}) collective-permute-start(bf16[256,256]{1,0:T(8,128)(2,1)S(1)} %gate.7.p0), channel_id=1, source_target_pairs={{0,1},{1,0},{2,3},{3,2},{4,5},{5,4},{6,7},{7,6},{8,9},{9,8},{10,11... | collective-permute-start | bytes 393224 | tf_op jit(solution)/shard_map/ppermute | solution.py:284
  64.5 0.0 collective-permute-done.9.refs_3_
  64.5 0.0 collective-permute-start.18
  64.5 3.4 %copy-done = bf16[4096,1024]{1,0:T(8,128)(2,1)S(1)} copy-done((bf16[4096,1024]{1,0:T(8,128)(2,1)S(1)}, bf16[4096,1024]{1,0:T(8,128)(2,1)}, u32[]{:S(2)}) %copy-start) | copy-done | bytes 8388632
  67.9 1.9 %project.4.acc_ref = f32[256,1024]{1,0:T(8,128)S(1)} custom-call(s32[4]{0:T(128)S(1)} %pad_add_fusion.order_ref, bf16[256,256]{1,0:T(8,128)(2,1)S(1)} %gate.4.refs_0_, bf16[256,256]{1,0:T(8,128)(2,1)S(1)} %collective-permute-done.7.refs_1_, bf16[256,256]{1,0:T(8,128)(2,1)S(1)} %collective-permute-done.8.refs_2_, ...), custom_call_target="tpu_custom_call" | custom-call | flops 536870912 | bytes 2097152 | tf_op jit(solution)/shard_map/project/pallas_call | solution.py:220
  69.7 0.0 collective-permute-done.12.p3
  69.8 1.5 %copy-done.1 = bf16[4096,1024]{1,0:T(8,128)(2,1)S(1)} copy-done((bf16[4096,1024]{1,0:T(8,128)(2,1)S(1)}, bf16[4096,1024]{1,0:T(8,128)(2,1)}, u32[]{:S(2)}) %copy-start.1) | copy-done | bytes 8388632
  71.3 1.9 %project.5.acc_ref = f32[256,1024]{1,0:T(8,128)S(1)} custom-call(s32[4]{0:T(128)S(1)} %pad_add_fusion.order_ref, f32[256,1024]{1,0:T(8,128)S(1)} %project.4.acc_ref, bf16[256,256]{1,0:T(8,128)(2,1)S(1)} %gate.5.p0, bf16[256,256]{1,0:T(8,128)(2,1)S(1)} %collective-permute-done.10.p1, bf16[256,256]{1,0:T(8,128)(2,1)S(1)} %collective-permute-done.11.p2, ...), custom_call_target="tpu_custom_call" | custom-call | flops 536870912 | bytes 2097152 | tf_op jit(solution)/shard_map/project/pallas_call | solution.py:220
  73.1 0.0 collective-permute-done.14.p2
  73.1 0.0 collective-permute-done.15.p3
  73.2 1.9 %project.6.acc_ref = f32[256,1024]{1,0:T(8,128)S(1)} custom-call(s32[4]{0:T(128)S(1)} %pad_add_fusion.order_ref, f32[256,1024]{1,0:T(8,128)S(1)} %project.5.acc_ref, bf16[256,256]{1,0:T(8,128)(2,1)S(1)} %gate.6.p0, bf16[256,256]{1,0:T(8,128)(2,1)S(1)} %collective-permute-done.13.p1, bf16[256,256]{1,0:T(8,128)(2,1)S(1)} %collective-permute-done.14.p2, ...), custom_call_target="tpu_custom_call" | custom-call | flops 536870912 | bytes 2097152 | tf_op jit(solution)/shard_map/project/pallas_call | solution.py:220
  75.0 0.0 collective-permute-done.17.p2
  75.0 0.0 collective-permute-done.18.p3
  75.1 2.7 %project.7 = bf16[256,1024]{1,0:T(8,128)(2,1)} custom-call(s32[4]{0:T(128)S(1)} %pad_add_fusion.order_ref, f32[256,1024]{1,0:T(8,128)S(1)} %project.6.acc_ref, bf16[256,256]{1,0:T(8,128)(2,1)S(1)} %gate.7.p0, bf16[256,256]{1,0:T(8,128)(2,1)S(1)} %collective-permute-done.16.p1, bf16[256,256]{1,0:T(8,128)(2,1)S(1)} %collective-permute-done.17.p2, ...), custom_call_target="tpu_custom_call" | custom-call | flops 536870912 | bytes 2097152 | tf_op jit(solution)/shard_map/project/pallas_call | solution.py:220
  (18 shorter events, 0.3 us)
Async XLA Ops:
  0.0 14.5 %copy-start.3 = (f32[1024,16]{0,1:T(8,128)S(1)}, f32[1024,16]{0,1:T(8,128)}, u32[]{:S(2)}) copy-start(f32[1024,16]{0,1:T(8,128)} %param.7) | copy-start | bytes 196612
  0.9 10.3 %collective-permute-start = (bf16[3,2,1024]{2,1,0:T(2,128)(2,1)S(1)}, bf16[3,2,1024]{2,1,0:T(2,128)(2,1)S(1)}, u32[]{:S(2)}, u32[]{:S(2)}) collective-permute-start(bf16[3,2,1024]{2,1,0:T(2,128)(2,1)S(1)} %get-tuple-element.10), channel_id=1, source_target_pairs={{0,4},{4,8},{8,12},{12,16},{16,20},{20,24},{24,28},{28,32},{32,36}... | collective-permute-start | bytes 36872 | tf_op jit(solution)/shard_map/ppermute | solution.py:265
  5.9 0.8 %copy-start.2 = (f32[1024,16]{0,1:T(8,128)S(1)}, f32[1024,16]{0,1:T(8,128)}, u32[]{:S(2)}) copy-start(f32[1024,16]{0,1:T(8,128)} %param.7) | copy-start | bytes 196612
  6.7 1.4 %copy-start.4 = (bf16[256,3,1024]{2,0,1:T(8,128)(2,1)S(1)}, bf16[256,3,1024]{2,0,1:T(8,128)(2,1)}, u32[]{:S(2)}) copy-start(bf16[256,3,1024]{2,0,1:T(8,128)(2,1)} %param.5) | copy-start | bytes 4718596
  8.2 0.8 %copy-start.7 = (f32[3,3,1024]{2,1,0:T(4,128)S(1)}, f32[3,3,1024]{2,1,0:T(4,128)}, u32[]{:S(2)}) copy-start(f32[3,3,1024]{2,1,0:T(4,128)} %taps_ref.3) | copy-start | bytes 110596
  9.0 30.0 %copy-start.5 = (bf16[256,3,1024]{2,0,1:T(8,128)(2,1)S(1)}, bf16[256,3,1024]{2,0,1:T(8,128)(2,1)}, u32[]{:S(2)}) copy-start(bf16[256,3,1024]{2,0,1:T(8,128)(2,1)} %param.5) | copy-start | bytes 4718596
  9.0 30.0 %copy-start.6 = (f32[1024,16]{0,1:T(8,128)S(1)}, f32[1024,16]{0,1:T(8,128)}, u32[]{:S(2)}) copy-start(f32[1024,16]{0,1:T(8,128)} %param.8) | copy-start | bytes 196612
  9.0 30.0 %copy-start.8 = (f32[3,3,1024]{2,1,0:T(4,128)S(1)}, f32[3,3,1024]{2,1,0:T(4,128)}, u32[]{:S(2)}) copy-start(f32[3,3,1024]{2,1,0:T(4,128)} %taps_ref.3) | copy-start | bytes 110596
  11.3 3.2 %collective-permute-start.1 = (f32[16,1024]{1,0:T(8,128)S(1)}, f32[16,1024]{1,0:T(8,128)S(1)}, u32[]{:S(2)}, u32[]{:S(2)}) collective-permute-start(f32[16,1024]{1,0:T(8,128)S(1)} %multiply_add_fusion), channel_id=1, source_target_pairs={{0,4},{4,0},{8,12},{12,8},{16,20},{20,16},{24,28},{28,24},{32,36},... | collective-permute-start | bytes 196616 | tf_op jit(solution)/shard_map/ppermute | solution.py:249
  14.6 5.6 %collective-permute-start.2 = (f32[16,1024]{1,0:T(8,128)S(1)}, f32[16,1024]{1,0:T(8,128)S(1)}, u32[]{:S(2)}, u32[]{:S(2)}) collective-permute-start(f32[16,1024]{1,0:T(8,128)S(1)} %add_select_fusion.4), channel_id=1, source_target_pairs={{0,12},{4,8},{8,4},{12,0},{16,28},{20,24},{24,20},{28,16},{32,44},... | collective-permute-start | bytes 196616 | tf_op jit(solution)/shard_map/ppermute | solution.py:249
  20.2 4.7 %collective-permute-start.3 = (f32[16,1024]{1,0:T(8,128)S(1)}, f32[16,1024]{1,0:T(8,128)S(1)}, u32[]{:S(2)}, u32[]{:S(2)}) collective-permute-start(f32[16,1024]{1,0:T(8,128)S(1)} %add_select_fusion.3), channel_id=1, source_target_pairs={{0,16},{4,20},{8,24},{12,28},{16,0},{20,4},{24,8},{28,12},{32,48},... | collective-permute-start | bytes 196616 | tf_op jit(solution)/shard_map/ppermute | solution.py:249
  24.9 3.7 %collective-permute-start.4 = (f32[16,1024]{1,0:T(8,128)S(1)}, f32[16,1024]{1,0:T(8,128)S(1)}, u32[]{:S(2)}, u32[]{:S(2)}) collective-permute-start(f32[16,1024]{1,0:T(8,128)S(1)} %add_select_fusion.2), channel_id=1, source_target_pairs={{0,32},{4,36},{8,40},{12,44},{16,48},{20,52},{24,56},{28,60},{32,0... | collective-permute-start | bytes 196616 | tf_op jit(solution)/shard_map/ppermute | solution.py:249
  28.6 4.8 %collective-permute-start.5 = (f32[16,1024]{1,0:T(8,128)S(1)}, f32[16,1024]{1,0:T(8,128)S(1)}, u32[]{:S(2)}, u32[]{:S(2)}) collective-permute-start(f32[16,1024]{1,0:T(8,128)S(1)} %add_select_fusion.1), channel_id=1, source_target_pairs={{0,64},{4,68},{8,72},{12,76},{16,80},{20,84},{24,88},{28,92},{32,9... | collective-permute-start | bytes 196616 | tf_op jit(solution)/shard_map/ppermute | solution.py:249
  33.4 9.2 %collective-permute-start.6 = (f32[16,1024]{1,0:T(8,128)S(1)}, f32[16,1024]{1,0:T(8,128)S(1)}, u32[]{:S(2)}, u32[]{:S(2)}) collective-permute-start(f32[16,1024]{1,0:T(8,128)S(1)} %add_select_fusion), channel_id=1, source_target_pairs={{0,224},{4,228},{8,232},{12,236},{16,240},{20,244},{24,248},{28,25... | collective-permute-start | bytes 196616 | tf_op jit(solution)/shard_map/ppermute | solution.py:249
  43.2 10.5 %collective-permute-start.8 = (bf16[256,256]{1,0:T(8,128)(2,1)S(1)}, bf16[256,256]{1,0:T(8,128)(2,1)S(1)}, u32[]{:S(2)}, u32[]{:S(2)}) collective-permute-start(bf16[256,256]{1,0:T(8,128)(2,1)S(1)} %gate.4.refs_0_), channel_id=1, source_target_pairs={{0,1},{1,0},{2,3},{3,2},{4,5},{5,4},{6,7},{7,6},{8,9},{9,8},{10,11... | collective-permute-start | bytes 393224 | tf_op jit(solution)/shard_map/ppermute | solution.py:284
  50.1 5.1 %collective-permute-start.7 = (bf16[256,256]{1,0:T(8,128)(2,1)S(1)}, bf16[256,256]{1,0:T(8,128)(2,1)S(1)}, u32[]{:S(2)}, u32[]{:S(2)}) collective-permute-start(bf16[256,256]{1,0:T(8,128)(2,1)S(1)} %gate.4.refs_0_), channel_id=1, source_target_pairs={{0,2},{1,3},{2,0},{3,1},{4,6},{5,7},{6,4},{7,5},{8,10},{9,11},{10,... | collective-permute-start | bytes 393224 | tf_op jit(solution)/shard_map/ppermute | solution.py:283
  50.9 5.7 %collective-permute-start.11 = (bf16[256,256]{1,0:T(8,128)(2,1)S(1)}, bf16[256,256]{1,0:T(8,128)(2,1)S(1)}, u32[]{:S(2)}, u32[]{:S(2)}) collective-permute-start(bf16[256,256]{1,0:T(8,128)(2,1)S(1)} %gate.5.p0), channel_id=1, source_target_pairs={{0,1},{1,0},{2,3},{3,2},{4,5},{5,4},{6,7},{7,6},{8,9},{9,8},{10,11... | collective-permute-start | bytes 393224 | tf_op jit(solution)/shard_map/ppermute | solution.py:284
  51.3 6.7 %collective-permute-start.10 = (bf16[256,256]{1,0:T(8,128)(2,1)S(1)}, bf16[256,256]{1,0:T(8,128)(2,1)S(1)}, u32[]{:S(2)}, u32[]{:S(2)}) collective-permute-start(bf16[256,256]{1,0:T(8,128)(2,1)S(1)} %gate.5.p0), channel_id=1, source_target_pairs={{0,2},{1,3},{2,0},{3,1},{4,6},{5,7},{6,4},{7,5},{8,10},{9,11},{10,... | collective-permute-start | bytes 393224 | tf_op jit(solution)/shard_map/ppermute | solution.py:283
  52.9 7.9 %collective-permute-start.13 = (bf16[256,256]{1,0:T(8,128)(2,1)S(1)}, bf16[256,256]{1,0:T(8,128)(2,1)S(1)}, u32[]{:S(2)}, u32[]{:S(2)}) collective-permute-start(bf16[256,256]{1,0:T(8,128)(2,1)S(1)} %gate.6.p0), channel_id=1, source_target_pairs={{0,2},{1,3},{2,0},{3,1},{4,6},{5,7},{6,4},{7,5},{8,10},{9,11},{10,... | collective-permute-start | bytes 393224 | tf_op jit(solution)/shard_map/ppermute | solution.py:283
  53.7 9.9 %collective-permute-start.16 = (bf16[256,256]{1,0:T(8,128)(2,1)S(1)}, bf16[256,256]{1,0:T(8,128)(2,1)S(1)}, u32[]{:S(2)}, u32[]{:S(2)}) collective-permute-start(bf16[256,256]{1,0:T(8,128)(2,1)S(1)} %gate.7.p0), channel_id=1, source_target_pairs={{0,2},{1,3},{2,0},{3,1},{4,6},{5,7},{6,4},{7,5},{8,10},{9,11},{10,... | collective-permute-start | bytes 393224 | tf_op jit(solution)/shard_map/ppermute | solution.py:283
  55.2 9.3 %collective-permute-start.9 = (bf16[256,256]{1,0:T(8,128)(2,1)S(1)}, bf16[256,256]{1,0:T(8,128)(2,1)S(1)}, u32[]{:S(2)}, u32[]{:S(2)}) collective-permute-start(bf16[256,256]{1,0:T(8,128)(2,1)S(1)} %collective-permute-done.7.refs_1_), channel_id=1, source_target_pairs={{0,1},{1,0},{2,3},{3,2},{4,5},{5,4},{6,7},{7,6},{8,9},{9,8},{10,11... | collective-permute-start | bytes 393224 | tf_op jit(solution)/shard_map/ppermute | solution.py:285
  56.5 16.6 %collective-permute-start.14 = (bf16[256,256]{1,0:T(8,128)(2,1)S(1)}, bf16[256,256]{1,0:T(8,128)(2,1)S(1)}, u32[]{:S(2)}, u32[]{:S(2)}) collective-permute-start(bf16[256,256]{1,0:T(8,128)(2,1)S(1)} %gate.6.p0), channel_id=1, source_target_pairs={{0,1},{1,0},{2,3},{3,2},{4,5},{5,4},{6,7},{7,6},{8,9},{9,8},{10,11... | collective-permute-start | bytes 393224 | tf_op jit(solution)/shard_map/ppermute | solution.py:284
  58.0 11.8 %collective-permute-start.12 = (bf16[256,256]{1,0:T(8,128)(2,1)S(1)}, bf16[256,256]{1,0:T(8,128)(2,1)S(1)}, u32[]{:S(2)}, u32[]{:S(2)}) collective-permute-start(bf16[256,256]{1,0:T(8,128)(2,1)S(1)} %collective-permute-done.10.p1), channel_id=1, source_target_pairs={{0,1},{1,0},{2,3},{3,2},{4,5},{5,4},{6,7},{7,6},{8,9},{9,8},{10,11... | collective-permute-start | bytes 393224 | tf_op jit(solution)/shard_map/ppermute | solution.py:285
  60.8 12.3 %collective-permute-start.15 = (bf16[256,256]{1,0:T(8,128)(2,1)S(1)}, bf16[256,256]{1,0:T(8,128)(2,1)S(1)}, u32[]{:S(2)}, u32[]{:S(2)}) collective-permute-start(bf16[256,256]{1,0:T(8,128)(2,1)S(1)} %collective-permute-done.13.p1), channel_id=1, source_target_pairs={{0,1},{1,0},{2,3},{3,2},{4,5},{5,4},{6,7},{7,6},{8,9},{9,8},{10,11... | collective-permute-start | bytes 393224 | tf_op jit(solution)/shard_map/ppermute | solution.py:285
  63.6 11.4 %collective-permute-start.17 = (bf16[256,256]{1,0:T(8,128)(2,1)S(1)}, bf16[256,256]{1,0:T(8,128)(2,1)S(1)}, u32[]{:S(2)}, u32[]{:S(2)}) collective-permute-start(bf16[256,256]{1,0:T(8,128)(2,1)S(1)} %gate.7.p0), channel_id=1, source_target_pairs={{0,1},{1,0},{2,3},{3,2},{4,5},{5,4},{6,7},{7,6},{8,9},{9,8},{10,11... | collective-permute-start | bytes 393224 | tf_op jit(solution)/shard_map/ppermute | solution.py:284
  64.5 10.6 %collective-permute-start.18 = (bf16[256,256]{1,0:T(8,128)(2,1)S(1)}, bf16[256,256]{1,0:T(8,128)(2,1)S(1)}, u32[]{:S(2)}, u32[]{:S(2)}) collective-permute-start(bf16[256,256]{1,0:T(8,128)(2,1)S(1)} %collective-permute-done.16.p1), channel_id=1, source_target_pairs={{0,1},{1,0},{2,3},{3,2},{4,5},{5,4},{6,7},{7,6},{8,9},{9,8},{10,11... | collective-permute-start | bytes 393224 | tf_op jit(solution)/shard_map/ppermute | solution.py:285
  64.5 3.4 %copy-start = (bf16[4096,1024]{1,0:T(8,128)(2,1)S(1)}, bf16[4096,1024]{1,0:T(8,128)(2,1)}, u32[]{:S(2)}) copy-start(bf16[4096,1024]{1,0:T(8,128)(2,1)} %w_ref.5) | copy-start | bytes 25165828
  67.9 3.4 %copy-start.1 = (bf16[4096,1024]{1,0:T(8,128)(2,1)S(1)}, bf16[4096,1024]{1,0:T(8,128)(2,1)}, u32[]{:S(2)}) copy-start(bf16[4096,1024]{1,0:T(8,128)(2,1)} %w_ref.5) | copy-start | bytes 25165828
where the time goes:
time: 78.1 us; the launch traced here: 77.7 us
  starting transfers between devices  36.7 us (47%)
  Pallas kernels  15.8 us (20%)
  waiting for transfers between devices  14.7 us (19%)
  local copies, waits for them, and re-layouts  9.78 us (13%)
    ppermute x6, starting transfers between devices, states_before(): other = lax.ppermute(total, 'ctx', list(enumerate(partner)))  17.3 us
    ppermute x6, waiting for transfers between devices, states_before(): other = lax.ppermute(total, 'ctx', list(enumerate(partner)))  10.2 us
    ppermute x4, starting transfers between devices, per_device(): beside = lax.ppermute(mine, 'chan', over_core)  8.27 us
    pallas_call x4, Pallas kernels, project(): pl.pallas_call(kernel, grid_spec=grid_spec, out_shape=jax.ShapeDtypeStruc...  8.26 us
    unnamed x20, local copies, waits for them, and re-layouts  7.95 us
    ppermute x4, waiting for transfers between devices, per_device(): across = lax.ppermute(mine, 'chan', over_x)  4.48 us
    ppermute x4, starting transfers between devices, per_device(): far = lax.ppermute(across, 'chan', over_core)  4.04 us
    ppermute x1, starting transfers between devices, per_device(): lax.ppermute(p[:, block - (TAPS - 1):], 'ctx', [(i, i + 1) for i in range...  4.03 us
  transfers between devices with their start and end apart: 19, of which 9 were waited for; matrix products, arithmetic and copies ran while one was open for 1% of the time, Pallas kernels for 16%

commit v1 on v0

v1 whole, which is shorter than its diff:
```python
import functools

import jax
import jax.numpy as jnp
from jax import lax
from jax.experimental import pallas as pl
from jax.experimental.pallas import tpu as pltpu
from jax.sharding import PartitionSpec as P

TAPS = 3
LANES = 128
ROWS = 8
INPUT_COST = 8 * 10**9
PARTS = (512, 512)
LOCAL_AT = 2
LOCAL_LIMIT = 50
INPUT_LIMIT = 52
LOAD_LIMIT = 38
HOLD = 9
VMEM = pl.BlockSpec(memory_space=pltpu.VMEM)
HBM = pl.BlockSpec(memory_space=pltpu.HBM)
SMEM = pl.BlockSpec(memory_space=pltpu.SMEM)


def params(mib):
    return pltpu.CompilerParams(vmem_limit_bytes=mib * 1024 * 1024)


def cost(flops, moved):
    return pl.CostEstimate(flops=flops, bytes_accessed=moved, transcendentals=0)


def short_filter(x_ref, tokens, taps, lanes):
    out = taps[0:1, lanes] * x_ref[pl.ds(ROWS, tokens), :]
    out = out + taps[1:2, lanes] * x_ref[pl.ds(ROWS - 1, tokens), :]
    return out + taps[2:3, lanes] * x_ref[pl.ds(ROWS - 2, tokens), :]


def input_kernel(p_hbm, taps_ref, u_ref, head_ref, taps_out, kv_ref, k_pad, v_pad, sems):
    block, channels = kv_ref.shape[1:]
    cblocks = channels // LANES
    copies = [pltpu.make_async_copy(p_hbm.at[1 + i], kv_ref.at[i], sems.at[i]) for i in range(2)]
    for copy in copies:
        copy.start()
    taps_out[...] = taps_ref[...]
    k_pad[pl.ds(0, ROWS), :] = jnp.zeros((ROWS, LANES), jnp.float32)
    v_pad[pl.ds(0, ROWS), :] = jnp.zeros((ROWS, LANES), jnp.float32)
    row = lax.broadcasted_iota(jnp.int32, (ROWS, LANES), 0)
    for copy in copies:
        copy.wait()
    for c in range(cblocks):
        lanes = pl.ds(c * LANES, LANES)
        k_pad[pl.ds(ROWS, block), :] = kv_ref[0, :, lanes].astype(jnp.float32)
        v_pad[pl.ds(ROWS, block), :] = kv_ref[1, :, lanes].astype(jnp.float32)
        head_ref[0, :, lanes] = k_pad[pl.ds(ROWS, TAPS - 1), :]
        head_ref[1, :, lanes] = v_pad[pl.ds(ROWS, TAPS - 1), :]
        u = short_filter(k_pad, block, taps_ref.at[1], lanes) * short_filter(v_pad, block, taps_ref.at[2], lanes)
        for j in range(block // ROWS):
            part = u[j * ROWS : (j + 1) * ROWS]
            u_ref[pl.ds((j * cblocks + c) * ROWS, ROWS), :] = part if j else jnp.where(row < TAPS - 1, 0.0, part)


def conv_input(p, taps):
    block, channels = p.shape[1:]
    padded = pltpu.VMEM((ROWS + block, LANES), jnp.float32)
    return pl.pallas_call(
        input_kernel,
        out_shape=(
            jax.ShapeDtypeStruct((block * channels // LANES, LANES), jnp.float32),
            jax.ShapeDtypeStruct((2, TAPS - 1, channels), jnp.float32),
            jax.ShapeDtypeStruct(taps.shape, taps.dtype),
        ),
        in_specs=[HBM, VMEM],
        out_specs=(VMEM,) * 3,
        scratch_shapes=[pltpu.VMEM((2, block, channels), p.dtype), padded, padded, pltpu.SemaphoreType.DMA((2,))],
        compiler_params=params(INPUT_LIMIT),
        cost_estimate=cost(INPUT_COST, 6 * block * channels),
        name="conv_input",
    )(p, taps)


def end_state_kernel(u_ref, rates_ref, res_ref, out_ref, tables_ref):
    modes, channels = rates_ref.shape
    cblocks = channels // LANES
    groups = u_ref.shape[0] // (cblocks * ROWS)
    row = lax.broadcasted_iota(jnp.int32, (ROWS, LANES), 0).astype(jnp.float32)
    tables_ref[0] = rates_ref[...]
    tables_ref[1] = res_ref[...]

    def lane_block(c, carry):
        lanes = pl.ds(pl.multiple_of(c * LANES, LANES), LANES)
        rates = [jnp.broadcast_to(rates_ref[m : m + 1, lanes], (ROWS, LANES)) for m in range(modes)]
        steps = [jnp.exp(-float(ROWS) * r) for r in rates]
        state = [u_ref[pl.ds(pl.multiple_of(c * ROWS, ROWS), ROWS), :]] * modes
        for j in range(1, groups):
            now = u_ref[pl.ds(pl.multiple_of((j * cblocks + c) * ROWS, ROWS), ROWS), :]
            state = [a * s + now for a, s in zip(steps, state)]
        for m in range(modes):
            weighted = state[m] * jnp.exp(rates[m] * (row - (ROWS - 1.0)))
            out_ref[m : m + 1, lanes] = jnp.sum(weighted, axis=0, keepdims=True)
        return carry

    lax.fori_loop(0, cblocks, lane_block, 0)


def end_state(u, rates, residues):
    return pl.pallas_call(
        end_state_kernel,
        out_shape=(
            jax.ShapeDtypeStruct(rates.shape, jnp.float32),
            jax.ShapeDtypeStruct((2, *rates.shape), jnp.float32),
        ),
        in_specs=[VMEM] * 3,
        out_specs=(VMEM,) * 2,
        compiler_params=params(8),
        cost_estimate=cost(2 * rates.shape[0] * u.size, 4 * u.size),
        name="end_state",
    )(u, rates, residues)


def local_kernel(p_hbm, prev_ref, taps_ref, tables_ref, in_ref, first_ref, y_ref, f_ref, q_ref, x_ref, u_ref, a_ref, r_ref, q_sem):
    block, channels = q_ref.shape
    modes = tables_ref.shape[1]
    cblocks = channels // LANES
    groups = block // ROWS
    q_copy = pltpu.make_async_copy(p_hbm.at[0], q_ref, q_sem)
    q_copy.start()
    u_ref[...] = in_ref[...]
    for c in range(cblocks):
        lanes = pl.ds(c * LANES, LANES)
        for t in range(TAPS - 1):
            u_ref[pl.ds(c * ROWS + t, 1), :] = first_ref[t : t + 1, lanes]
        for m in range(0, modes, ROWS):
            rows = pl.ds(m * cblocks + c, ROWS, stride=cblocks)
            a_ref[rows, :] = jnp.exp(-tables_ref[0, m : m + ROWS, lanes])
            r_ref[rows, :] = tables_ref[1, m : m + ROWS, lanes]

    def group(j, state):
        state = list(state)
        for i in range(ROWS):
            at = pl.ds(j * ROWS * cblocks + i, cblocks, stride=ROWS)
            now = u_ref[at, :]
            total = [None] * 4
            for m in range(modes):
                a = a_ref[pl.ds(m * cblocks, cblocks), :]
                r = r_ref[pl.ds(m * cblocks, cblocks), :]
                state[m] = a * state[m] + now
                term = r * state[m]
                total[m % 4] = term if total[m % 4] is None else total[m % 4] + term
            y_ref[at, :] = (total[0] + total[1]) + (total[2] + total[3])
        return tuple(state)

    lax.fori_loop(0, groups, group, (jnp.zeros((cblocks, LANES), jnp.float32),) * modes)
    q_copy.wait()
    for c in range(cblocks):
        lanes = pl.ds(c * LANES, LANES)
        x_ref[pl.ds(ROWS - 2, 2), :] = prev_ref[0, :, lanes].astype(jnp.float32)
        x_ref[pl.ds(ROWS, block), :] = q_ref[:, lanes].astype(jnp.float32)
        feature = short_filter(x_ref, block, taps_ref.at[0], lanes)
        for j in range(groups):
            f_ref[pl.ds((j * cblocks + c) * ROWS, ROWS), :] = feature[j * ROWS : (j + 1) * ROWS]


def local_part(p, prev, taps, tables, u, first):
    block, channels = p.shape[1:]
    modes = tables.shape[1]
    cblocks = channels // LANES
    table = pltpu.VMEM((modes * cblocks, LANES), jnp.float32)
    tiled = jax.ShapeDtypeStruct((block * cblocks, LANES), jnp.float32)
    return pl.pallas_call(
        local_kernel,
        out_shape=(tiled, tiled),
        in_specs=[HBM] + [VMEM] * 5,
        out_specs=(VMEM, VMEM),
        scratch_shapes=[
            pltpu.VMEM((block, channels), p.dtype),
            pltpu.VMEM((ROWS + block, LANES), jnp.float32),
            pltpu.VMEM((block * cblocks, LANES), jnp.float32),
            table,
            table,
            pltpu.SemaphoreType.DMA,
        ],
        compiler_params=params(LOCAL_LIMIT),
        cost_estimate=cost(4 * modes * block * channels, 6 * block * channels),
        name="local_part",
    )(p, prev, taps, tables, u, first)


def gate_kernel(first, y_ref, f_ref, state_ref, tables_ref, out_ref):
    modes = tables_ref.shape[1]
    cblocks = tables_ref.shape[2] // LANES
    row = lax.broadcasted_iota(jnp.int32, (ROWS, LANES), 0).astype(jnp.float32)
    for c in range(out_ref.shape[1] // LANES):
        block = first // LANES + c
        lanes = pl.ds(first + c * LANES, LANES)
        terms, steps = [], []
        for m in range(modes):
            rate = jnp.broadcast_to(tables_ref[0, m : m + 1, lanes], (ROWS, LANES))
            scale = tables_ref[1, m : m + 1, lanes] * state_ref[m : m + 1, lanes]
            terms.append(jnp.exp(-rate * (row + 1.0)) * scale)
            steps.append(jnp.exp(-float(ROWS) * rate))

        def pair(jj, terms):
            terms = list(terms)
            both = []
            for half in range(2):
                at = pl.ds(pl.multiple_of(((2 * jj + half) * cblocks + block) * ROWS, ROWS), ROWS)
                total = [y_ref[at, :], None, None, None]
                for m in range(modes):
                    total[m % 4] = terms[m] if total[m % 4] is None else total[m % 4] + terms[m]
                    terms[m] = terms[m] * steps[m]
                both.append(f_ref[at, :] * ((total[0] + total[1]) + (total[2] + total[3])))
            rows = pl.ds(pl.multiple_of(jj * 2 * ROWS, 2 * ROWS), 2 * ROWS)
            out_ref[rows, pl.ds(c * LANES, LANES)] = jnp.concatenate(both, axis=0).astype(out_ref.dtype)
            return tuple(terms)

        lax.fori_loop(0, out_ref.shape[0] // (2 * ROWS), pair, tuple(terms), unroll=4)


def gate(first, last, y, f, state, tables):
    modes, channels = tables.shape[1:]
    block = y.shape[0] * LANES // channels
    size = block * (last - first)
    return pl.pallas_call(
        functools.partial(gate_kernel, first),
        out_shape=jax.ShapeDtypeStruct((block, last - first), jnp.bfloat16),
        in_specs=[VMEM] * 4,
        out_specs=VMEM,
        compiler_params=params(4),
        cost_estimate=cost(2 * modes * size, 6 * size),
        name="gate",
    )(y, f, state, tables)


def load_kernel(order_ref, w_hbm, *refs):
    rows_refs, sems = refs[:4], refs[4]
    depth = w_hbm.shape[0] // 4
    copies = []
    for number, rows_ref in enumerate(rows_refs):
        rows = pl.ds(pl.multiple_of(order_ref[number] * depth, depth), depth)
        copies.append(pltpu.make_async_copy(w_hbm.at[rows, :], rows_ref, sems.at[number]))
        copies[-1].start()
    for copy in copies:
        copy.wait()


def load_rows(order, weight):
    depth, features = weight.shape[0] // 4, weight.shape[1]
    return pl.pallas_call(
        load_kernel,
        out_shape=[jax.ShapeDtypeStruct((depth, features), weight.dtype)] * 4,
        in_specs=[SMEM, HBM],
        out_specs=[VMEM] * 4,
        scratch_shapes=[pltpu.SemaphoreType.DMA((4,))],
        compiler_params=params(LOAD_LIMIT),
        cost_estimate=cost(0, 2 * weight.size),
        name="load_rows",
    )(order, weight)


def project_kernel(first, has_acc, *refs):
    count = 4
    pieces, loaded, out_ref = refs[:count], refs[count : 2 * count], refs[-1]
    total = refs[2 * count][...] if has_acc else None
    for piece, rows_ref in zip(pieces, loaded):
        rows = rows_ref[pl.ds(first, piece.shape[1]), :]
        term = jnp.dot(piece[...], rows, preferred_element_type=jnp.float32)
        total = term if total is None else total + term
    out_ref[...] = total.astype(out_ref.dtype)


def project(pieces, loaded, first, acc, kind):
    block, features = pieces[0].shape[0], loaded[0].shape[1]
    extra = [] if acc is None else [acc]
    return pl.pallas_call(
        functools.partial(project_kernel, first, len(extra)),
        out_shape=jax.ShapeDtypeStruct((block, features), kind),
        in_specs=[VMEM] * (len(pieces) + len(loaded) + len(extra)),
        out_specs=VMEM,
        compiler_params=params(8),
        cost_estimate=cost(0, 1024),
        name="project",
    )(*pieces, *loaded, *extra)


def partners(count):
    levels, size = [], 1
    while size < count:
        if size in (2, 32):
            ring = 4 if size == 2 else 8
            unit = size * 2 // ring
            flip = lambda i: (i // (unit * ring)) * unit * ring + (ring - 1 - i // unit % ring) * unit + i % unit
        else:
            flip = lambda i: i ^ size
        levels.append((size, [flip(i) for i in range(count)]))
        size *= 2
    return levels


def tied(value, *others):
    return lax.optimization_barrier((value, *others))[0]


def per_device(projected, short_taps, decay_rates, residues, out_weight):
    block, _, channels = projected.shape
    count = lax.axis_size("ctx")
    position = lax.axis_index("ctx")
    own = lax.axis_index("chan")
    order = jnp.stack([own, own ^ 1, own ^ 2, own ^ 3]).astype(jnp.int32)
    over_x = lambda value: lax.ppermute(value, "chan", [(i, i ^ 2) for i in range(4)])
    over_core = lambda value: lax.ppermute(value, "chan", [(i, i ^ 1) for i in range(4)])

    p = projected.transpose(1, 0, 2)
    prev = lax.ppermute(p[:, block - (TAPS - 1) :], "ctx", [(i, i + 1) for i in range(count - 1)])
    u, head, taps = conv_input(p, short_taps)
    total, tables = end_state(u, decay_rates.T, residues.T)
    rates = tables[0]
    head = jnp.concatenate([prev[1:].astype(jnp.float32), head], axis=1)
    feats = sum(taps[1:, j, None] * head[:, TAPS - 1 - j : 2 * (TAPS - 1) - j] for j in range(TAPS))
    first = feats[0] * feats[1]
    for t in range(TAPS - 1):
        total = total + jnp.exp(-rates * float(block - 1 - t)) * first[t][None]

    before = jnp.zeros_like(total)
    due = ()
    for level, (size, partner) in enumerate(partners(count)):
        total, before, *_ = lax.optimization_barrier((total, before, *due))
        due = ()
        other = lax.ppermute(total, "ctx", list(enumerate(partner)))
        if level == LOCAL_AT:
            y, f = local_part(p, prev, taps, tables, u, tied(first, total))
            due = (y,)
        later = (position // size) % 2 == 1
        offset = (position % size).astype(jnp.float32)
        decay = jnp.exp(-rates * (block * offset))
        before = before + jnp.where(later, other * decay, 0.0)
        whole = jnp.exp(-rates * float(block * size))
        total = jnp.where(later, other * whole + total, total * whole + other)

    acc, start, loaded, accs = None, 0, None, []
    for number, width in enumerate(PARTS):
        mine = gate(start, start + width, y, f, before, tables)
        if loaded is None:
            loaded = load_rows(tied(order, mine), out_weight)
        across, beside = over_x(mine), over_core(mine)
        hold = loaded[:1] if number == 0 else accs[: number - HOLD + 1][-1:] if number >= HOLD else ()
        far = over_core(tied(across, *hold) if hold else across)
        kind = jnp.float32 if start + width < channels else jnp.bfloat16
        acc = project((mine, beside, across, far), loaded, start, acc, kind)
        accs.append(acc)
        start += width
    return acc


def solution(mesh):
    in_specs = (
        P("ctx", None, "chan"),
        P(None, None, "chan"),
        P("chan", None),
        P("chan", None),
        P(None, "chan"),
    )
    return jax.shard_map(
        per_device, mesh=mesh, in_specs=in_specs, out_specs=P("ctx", "chan"), check_vma=False
    )
```

time: 78.1 us -> 61.5 us (0.79)
  local copies, waits for them, and re-layouts: 9.78 us -> 1.67 us
  waiting for transfers between devices: 14.7 us -> 9.25 us
  starting transfers between devices: 36.7 us -> 34.3 us
    unnamed x20 -> x8, local copies, waits for them, and re-layouts: 7.95 us -> 0.82 us
    ppermute x18 -> x12, waiting for transfers between devices: 14.7 us -> 9.25 us  [the longest x6 9.23 us: per_device(): other = lax.ppermute(total, 'ctx', list(enumerate(partner)))]
    ppermute x18 -> x12, starting transfers between devices: 32.7 us -> 30.1 us  [the longest x6 17.7 us: per_device(): other = lax.ppermute(total, 'ctx', list(enumerate(partner)))]
    slice x3, local copies, waits for them, and re-layouts: 1.83 us -> 0.84 us  [the longest x1 0.81 us: per_device(): p[:, block - (TAPS - 1):]]
    pallas_call x10 -> x8, Pallas kernels: 15.8 us -> 15.4 us  [the longest x1 4.05 us: load_rows(): pl.pallas_call(load_kernel, out_shape=[jax.ShapeDtypeStruct((depth, featu...]
  transfers between devices with their start and end apart: 19 -> 13, of which waited for: 9 -> 5; matrix products, arithmetic and copies ran while one was open for 1% -> 0% of each run, Pallas kernels for 16% -> 21%
where the time goes in v1:
time: 61.5 us; the launch traced here: 61.2 us
  starting transfers between devices  34.3 us (56%)
  Pallas kernels  15.4 us (25%)
  waiting for transfers between devices  9.25 us (15%)
  local copies, waits for them, and re-layouts  1.67 us (3%)
    ppermute x6, starting transfers between devices, per_device(): other = lax.ppermute(total, 'ctx', list(enumerate(partner)))  17.7 us
    ppermute x4, starting transfers between devices, per_device(): lax.ppermute(value, 'chan', [(i, i ^ 1) for i in range(4)])  10.8 us
    ppermute x6, waiting for transfers between devices, per_device(): other = lax.ppermute(total, 'ctx', list(enumerate(partner)))  9.23 us
    ppermute x1, starting transfers between devices, per_device(): lax.ppermute(p[:, block - (TAPS - 1):], 'ctx', [(i, i + 1) for i in range...  4.16 us
    pallas_call x1, Pallas kernels, load_rows(): pl.pallas_call(load_kernel, out_shape=[jax.ShapeDtypeStruct((depth, featu...  4.05 us
    pallas_call x2, Pallas kernels, project(): pl.pallas_call(functools.partial(project_kernel, first, len(extra)), out_...  3.42 us
    pallas_call x1, Pallas kernels, local_part(): pl.pallas_call(local_kernel, out_shape=(tiled, tiled), in_specs=[HBM] + [...  2.99 us
    pallas_call x1, Pallas kernels, conv_input(): pl.pallas_call(input_kernel, out_shape=(jax.ShapeDtypeStruct((block * cha...  2.03 us
  transfers between devices with their start and end apart: 13, of which 5 were waited for; matrix products, arithmetic and copies ran while one was open for 0% of the time, Pallas kernels for 21%

profile of v1, /device:TPU:1, one launch (start us, length us, event | category | flops | bytes accessed | tf_op | source)
XLA Modules:
  0.0 61.2 jit_solution(767262146539377553)
XLA Ops:
  0.0 0.8 %slice.46 = bf16[3,2,1024]{2,1,0:T(2,128)(2,1)S(1)} slice(bf16[3,256,1024]{2,1,0:T(8,128)(2,1)} %bitcast.121), slice={[0:3], [254:256], [0:1024]} | slice | bytes 24576 | tf_op jit(solution)/shard_map/slice | solution.py:314
  0.8 0.0 copy-start
  0.8 0.0 copy-start.1
  0.8 4.2 %collective-permute-start = (bf16[3,2,1024]{2,1,0:T(2,128)(2,1)S(1)}, bf16[3,2,1024]{2,1,0:T(2,128)(2,1)S(1)}, u32[]{:S(2)}, u32[]{:S(2)}) collective-permute-start(bf16[3,2,1024]{2,1,0:T(2,128)(2,1)S(1)} %slice.46), channel_id=1, source_target_pairs={{0,4},{4,8},{8,12},{12,16},{16,20},{20,24},{24,28},{28,32},{32,36}... | collective-permute-start | bytes 36872 | tf_op jit(solution)/shard_map/ppermute | solution.py:314
  5.0 0.0 copy-start.2
  5.0 0.8 %copy-done.2 = f32[3,3,1024]{2,1,0:T(4,128)S(1)} copy-done((f32[3,3,1024]{2,1,0:T(4,128)S(1)}, f32[3,3,1024]{2,1,0:T(4,128)}, u32[]{:S(2)}) %copy-start.2) | copy-done | bytes 36888
  5.8 2.0 %conv_input.1 = (f32[2048,128]{1,0:T(8,128)S(1)}, f32[2,2,1024]{2,1,0:T(2,128)S(1)}, f32[3,3,1024]{2,1,0:T(4,128)S(1)}) custom-call(bf16[3,256,1024]{2,1,0:T(8,128)(2,1)} %bitcast.122, f32[3,3,1024]{2,1,0:T(4,128)S(1)} %copy-done.2), custom_call_target="tpu_custom_call" | custom-call | flops 8000000000 | bytes 1572864 | tf_op jit(solution)/shard_map/conv_input/pallas_call | solution.py:66
  7.9 0.0 copy-done
  7.9 0.0 copy-done.1
  7.9 1.4 %end_state.1 = (f32[16,1024]{1,0:T(8,128)S(1)}, f32[2,16,1024]{2,1,0:T(8,128)S(1)}) custom-call(f32[2048,128]{1,0:T(8,128)S(1)} %get-tuple-element.32.u_ref.in_ref, f32[16,1024]{1,0:T(8,128)S(1)} %bitcast.119, f32[16,1024]{1,0:T(8,128)S(1)} %bitcast.120), custom_call_target="tpu_custom_call" | custom-call | flops 8388608 | bytes 1048576 | tf_op jit(solution)/shard_map/end_state/pallas_call | solution.py:107
  9.4 0.0 collective-permute-done.prev_ref
  9.5 1.4 %collective-permute-start.1 = (f32[16,1024]{1,0:T(8,128)S(1)}, f32[16,1024]{1,0:T(8,128)S(1)}, u32[]{:S(2)}, u32[]{:S(2)}) collective-permute-start(f32[16,1024]{1,0:T(8,128)S(1)} %fusion.27), channel_id=1, source_target_pairs={{0,4},{4,0},{8,12},{12,8},{16,20},{20,16},{24,28},{28,24},{32,36},... | collective-permute-start | bytes 196616 | tf_op jit(solution)/shard_map/ppermute | solution.py:329
  10.9 1.8 %collective-permute-done.1 = f32[16,1024]{1,0:T(8,128)S(1)} collective-permute-done((f32[16,1024]{1,0:T(8,128)S(1)}, f32[16,1024]{1,0:T(8,128)S(1)}, u32[]{:S(2)}, u32[]{:S(2)}) %collective-permute-start.1) | collective-permute-done | bytes 65568 | tf_op jit(solution)/shard_map/ppermute | solution.py:329
  12.8 3.9 %collective-permute-start.2 = (f32[16,1024]{1,0:T(8,128)S(1)}, f32[16,1024]{1,0:T(8,128)S(1)}, u32[]{:S(2)}, u32[]{:S(2)}) collective-permute-start(f32[16,1024]{1,0:T(8,128)S(1)} %get-tuple-element.38), channel_id=1, source_target_pairs={{0,12},{4,8},{8,4},{12,0},{16,28},{20,24},{24,20},{28,16},{32,44},... | collective-permute-start | bytes 196616 | tf_op jit(solution)/shard_map/ppermute | solution.py:329
  16.7 1.7 %collective-permute-done.2 = f32[16,1024]{1,0:T(8,128)S(1)} collective-permute-done((f32[16,1024]{1,0:T(8,128)S(1)}, f32[16,1024]{1,0:T(8,128)S(1)}, u32[]{:S(2)}, u32[]{:S(2)}) %collective-permute-start.2) | collective-permute-done | bytes 65568 | tf_op jit(solution)/shard_map/ppermute | solution.py:329
  18.4 2.1 %collective-permute-start.3 = (f32[16,1024]{1,0:T(8,128)S(1)}, f32[16,1024]{1,0:T(8,128)S(1)}, u32[]{:S(2)}, u32[]{:S(2)}) collective-permute-start(f32[16,1024]{1,0:T(8,128)S(1)} %get-tuple-element.40), channel_id=1, source_target_pairs={{0,16},{4,20},{8,24},{12,28},{16,0},{20,4},{24,8},{28,12},{32,48},... | collective-permute-start | bytes 196616 | tf_op jit(solution)/shard_map/ppermute | solution.py:329
  20.5 3.0 %local_part.1 = (f32[2048,128]{1,0:T(8,128)S(1)}, f32[2048,128]{1,0:T(8,128)S(1)}) custom-call(bf16[3,256,1024]{2,1,0:T(8,128)(2,1)} %bitcast.123, bf16[3,2,1024]{2,1,0:T(2,128)(2,1)S(1)} %collective-permute-done.prev_ref, f32[3,3,1024]{2,1,0:T(4,128)S(1)} %get-tuple-element.31.taps_ref, f32[2,16,1024]{2,1,0:T(8,128)S(1)} %get-tuple-element.33.tables_ref, ...), custom_call_target="tpu_custom_call" | custom-call | flops 16777216 | bytes 1572864 | tf_op jit(solution)/shard_map/local_part/pallas_call | solution.py:170
  23.5 0.0 collective-permute-done.3
  23.6 1.7 %collective-permute-start.4 = (f32[16,1024]{1,0:T(8,128)S(1)}, f32[16,1024]{1,0:T(8,128)S(1)}, u32[]{:S(2)}, u32[]{:S(2)}) collective-permute-start(f32[16,1024]{1,0:T(8,128)S(1)} %get-tuple-element.45), channel_id=1, source_target_pairs={{0,32},{4,36},{8,40},{12,44},{16,48},{20,52},{24,56},{28,60},{32,0... | collective-permute-start | bytes 196616 | tf_op jit(solution)/shard_map/ppermute | solution.py:329
  25.3 1.7 %collective-permute-done.4 = f32[16,1024]{1,0:T(8,128)S(1)} collective-permute-done((f32[16,1024]{1,0:T(8,128)S(1)}, f32[16,1024]{1,0:T(8,128)S(1)}, u32[]{:S(2)}, u32[]{:S(2)}) %collective-permute-start.4) | collective-permute-done | bytes 65568 | tf_op jit(solution)/shard_map/ppermute | solution.py:329
  27.0 4.1 %collective-permute-start.5 = (f32[16,1024]{1,0:T(8,128)S(1)}, f32[16,1024]{1,0:T(8,128)S(1)}, u32[]{:S(2)}, u32[]{:S(2)}) collective-permute-start(f32[16,1024]{1,0:T(8,128)S(1)} %get-tuple-element.47), channel_id=1, source_target_pairs={{0,64},{4,68},{8,72},{12,76},{16,80},{20,84},{24,88},{28,92},{32,9... | collective-permute-start | bytes 196616 | tf_op jit(solution)/shard_map/ppermute | solution.py:329
  31.1 1.7 %collective-permute-done.5 = f32[16,1024]{1,0:T(8,128)S(1)} collective-permute-done((f32[16,1024]{1,0:T(8,128)S(1)}, f32[16,1024]{1,0:T(8,128)S(1)}, u32[]{:S(2)}, u32[]{:S(2)}) %collective-permute-start.5) | collective-permute-done | bytes 65568 | tf_op jit(solution)/shard_map/ppermute | solution.py:329
  32.9 4.4 %collective-permute-start.6 = (f32[16,1024]{1,0:T(8,128)S(1)}, f32[16,1024]{1,0:T(8,128)S(1)}, u32[]{:S(2)}, u32[]{:S(2)}) collective-permute-start(f32[16,1024]{1,0:T(8,128)S(1)} %get-tuple-element.50), channel_id=1, source_target_pairs={{0,224},{4,228},{8,232},{12,236},{16,240},{20,244},{24,248},{28,25... | collective-permute-start | bytes 196616 | tf_op jit(solution)/shard_map/ppermute | solution.py:329
  37.3 2.4 %collective-permute-done.6 = f32[16,1024]{1,0:T(8,128)S(1)} collective-permute-done((f32[16,1024]{1,0:T(8,128)S(1)}, f32[16,1024]{1,0:T(8,128)S(1)}, u32[]{:S(2)}, u32[]{:S(2)}) %collective-permute-start.6) | collective-permute-done | bytes 65568 | tf_op jit(solution)/shard_map/ppermute | solution.py:329
  39.7 0.8 %gate.3.refs_0_ = bf16[256,512]{1,0:T(8,128)(2,1)S(1)} custom-call(f32[2048,128]{1,0:T(8,128)S(1)} %get-tuple-element.42.y_ref, f32[2048,128]{1,0:T(8,128)S(1)} %get-tuple-element.43.f_ref, f32[16,1024]{1,0:T(8,128)S(1)} %fusion.1.state_ref, f32[2,16,1024]{2,1,0:T(8,128)S(1)} %get-tuple-element.33.tables_ref), custom_call_target="tpu_custom_call" | custom-call | flops 4194304 | bytes 786432 | tf_op jit(solution)/shard_map/gate/pallas_call | solution.py:224
  40.5 0.4 collective-permute-start.11
  40.8 0.8 %gate.2.refs_0_ = bf16[256,512]{1,0:T(8,128)(2,1)S(1)} custom-call(f32[2048,128]{1,0:T(8,128)S(1)} %get-tuple-element.42.y_ref, f32[2048,128]{1,0:T(8,128)S(1)} %get-tuple-element.43.f_ref, f32[16,1024]{1,0:T(8,128)S(1)} %fusion.1.state_ref, f32[2,16,1024]{2,1,0:T(8,128)S(1)} %get-tuple-element.33.tables_ref), custom_call_target="tpu_custom_call" | custom-call | flops 4194304 | bytes 786432 | tf_op jit(solution)/shard_map/gate/pallas_call | solution.py:224
  41.6 1.3 %collective-permute-start.8 = (bf16[256,512]{1,0:T(8,128)(2,1)S(1)}, bf16[256,512]{1,0:T(8,128)(2,1)S(1)}, u32[]{:S(2)}, u32[]{:S(2)}) collective-permute-start(bf16[256,512]{1,0:T(8,128)(2,1)S(1)} %gate.2.refs_0_), channel_id=1, source_target_pairs={{0,2},{1,3},{2,0},{3,1},{4,6},{5,7},{6,4},{7,5},{8,10},{9,11},{10,... | collective-permute-start | bytes 786440 | tf_op jit(solution)/shard_map/ppermute | solution.py:310
  42.9 0.1 pad_add_fusion.order_ref
  43.0 8.6 %collective-permute-start.10 = (bf16[256,512]{1,0:T(8,128)(2,1)S(1)}, bf16[256,512]{1,0:T(8,128)(2,1)S(1)}, u32[]{:S(2)}, u32[]{:S(2)}) collective-permute-start(bf16[256,512]{1,0:T(8,128)(2,1)S(1)} %gate.3.refs_0_), channel_id=1, source_target_pairs={{0,1},{1,0},{2,3},{3,2},{4,5},{5,4},{6,7},{7,6},{8,9},{9,8},{10,11... | collective-permute-start | bytes 786440 | tf_op jit(solution)/shard_map/ppermute | solution.py:311
  51.6 4.0 %load_rows.1 = (bf16[1024,1024]{1,0:T(8,128)(2,1)S(1)}, bf16[1024,1024]{1,0:T(8,128)(2,1)S(1)}, bf16[1024,1024]{1,0:T(8,128)(2,1)S(1)}, bf16[1024,1024]{1,0:T(8,128)(2,1)S(1)}) custom-call(s32[4]{0:T(128)S(1)} %pad_add_fusion.order_ref, bf16[4096,1024]{1,0:T(8,128)(2,1)} %w_hbm.1), custom_call_target="tpu_custom_call" | custom-call | bytes 8388608 | tf_op jit(solution)/shard_map/load_rows/pallas_call | solution.py:249
  55.6 0.0 collective-permute-done.11.refs_2_
  55.7 0.1 collective-permute-start.12
  55.8 0.5 collective-permute-start.7
  56.3 0.0 collective-permute-done.8.refs_2_
  56.3 1.5 %collective-permute-start.9 = (bf16[256,512]{1,0:T(8,128)(2,1)S(1)}, bf16[256,512]{1,0:T(8,128)(2,1)S(1)}, u32[]{:S(2)}, u32[]{:S(2)}) collective-permute-start(bf16[256,512]{1,0:T(8,128)(2,1)S(1)} %collective-permute-done.8.refs_2_), channel_id=1, source_target_pairs={{0,1},{1,0},{2,3},{3,2},{4,5},{5,4},{6,7},{7,6},{8,9},{9,8},{10,11... | collective-permute-start | bytes 786440 | tf_op jit(solution)/shard_map/ppermute | solution.py:311
  57.8 0.0 collective-permute-done.10.refs_1_
  57.8 0.0 collective-permute-done.12.refs_3_
  57.8 1.3 %project.2.refs_8_ = f32[256,1024]{1,0:T(8,128)S(1)} custom-call(bf16[256,512]{1,0:T(8,128)(2,1)S(1)} %gate.3.refs_0_, bf16[256,512]{1,0:T(8,128)(2,1)S(1)} %collective-permute-done.10.refs_1_, bf16[256,512]{1,0:T(8,128)(2,1)S(1)} %collective-permute-done.11.refs_2_, bf16[256,512]{1,0:T(8,128)(2,1)S(1)} %collective-permute-done.12.refs_3_, ...), custom_call_target="tpu_custom_call" | custom-call | bytes 1024 | tf_op jit(solution)/shard_map/project/pallas_call | solution.py:275
  59.1 0.0 collective-permute-done.7.refs_1_
  59.1 0.0 collective-permute-done.9.refs_3_
  59.1 2.1 %project.3 = bf16[256,1024]{1,0:T(8,128)(2,1)} custom-call(bf16[256,512]{1,0:T(8,128)(2,1)S(1)} %gate.2.refs_0_, bf16[256,512]{1,0:T(8,128)(2,1)S(1)} %collective-permute-done.7.refs_1_, bf16[256,512]{1,0:T(8,128)(2,1)S(1)} %collective-permute-done.8.refs_2_, bf16[256,512]{1,0:T(8,128)(2,1)S(1)} %collective-permute-done.9.refs_3_, ...), custom_call_target="tpu_custom_call" | custom-call | bytes 1024 | tf_op jit(solution)/shard_map/project/pallas_call | solution.py:275
  (16 shorter events, 0.4 us)
Async XLA Ops:
  0.8 7.1 %copy-start = (f32[1024,16]{0,1:T(8,128)S(1)}, f32[1024,16]{0,1:T(8,128)}, u32[]{:S(2)}) copy-start(f32[1024,16]{0,1:T(8,128)} %param.7) | copy-start | bytes 196612
  0.8 7.1 %copy-start.1 = (f32[1024,16]{0,1:T(8,128)S(1)}, f32[1024,16]{0,1:T(8,128)}, u32[]{:S(2)}) copy-start(f32[1024,16]{0,1:T(8,128)} %param.8) | copy-start | bytes 196612
  0.8 8.5 %collective-permute-start = (bf16[3,2,1024]{2,1,0:T(2,128)(2,1)S(1)}, bf16[3,2,1024]{2,1,0:T(2,128)(2,1)S(1)}, u32[]{:S(2)}, u32[]{:S(2)}) collective-permute-start(bf16[3,2,1024]{2,1,0:T(2,128)(2,1)S(1)} %slice.46), channel_id=1, source_target_pairs={{0,4},{4,8},{8,12},{12,16},{16,20},{20,24},{24,28},{28,32},{32,36}... | collective-permute-start | bytes 36872 | tf_op jit(solution)/shard_map/ppermute | solution.py:314
  5.0 0.8 %copy-start.2 = (f32[3,3,1024]{2,1,0:T(4,128)S(1)}, f32[3,3,1024]{2,1,0:T(4,128)}, u32[]{:S(2)}) copy-start(f32[3,3,1024]{2,1,0:T(4,128)} %taps_ref.1) | copy-start | bytes 110596
  9.5 3.2 %collective-permute-start.1 = (f32[16,1024]{1,0:T(8,128)S(1)}, f32[16,1024]{1,0:T(8,128)S(1)}, u32[]{:S(2)}, u32[]{:S(2)}) collective-permute-start(f32[16,1024]{1,0:T(8,128)S(1)} %fusion.27), channel_id=1, source_target_pairs={{0,4},{4,0},{8,12},{12,8},{16,20},{20,16},{24,28},{28,24},{32,36},... | collective-permute-start | bytes 196616 | tf_op jit(solution)/shard_map/ppermute | solution.py:329
  12.8 5.6 %collective-permute-start.2 = (f32[16,1024]{1,0:T(8,128)S(1)}, f32[16,1024]{1,0:T(8,128)S(1)}, u32[]{:S(2)}, u32[]{:S(2)}) collective-permute-start(f32[16,1024]{1,0:T(8,128)S(1)} %get-tuple-element.38), channel_id=1, source_target_pairs={{0,12},{4,8},{8,4},{12,0},{16,28},{20,24},{24,20},{28,16},{32,44},... | collective-permute-start | bytes 196616 | tf_op jit(solution)/shard_map/ppermute | solution.py:329
  18.4 5.1 %collective-permute-start.3 = (f32[16,1024]{1,0:T(8,128)S(1)}, f32[16,1024]{1,0:T(8,128)S(1)}, u32[]{:S(2)}, u32[]{:S(2)}) collective-permute-start(f32[16,1024]{1,0:T(8,128)S(1)} %get-tuple-element.40), channel_id=1, source_target_pairs={{0,16},{4,20},{8,24},{12,28},{16,0},{20,4},{24,8},{28,12},{32,48},... | collective-permute-start | bytes 196616 | tf_op jit(solution)/shard_map/ppermute | solution.py:329
  23.6 3.4 %collective-permute-start.4 = (f32[16,1024]{1,0:T(8,128)S(1)}, f32[16,1024]{1,0:T(8,128)S(1)}, u32[]{:S(2)}, u32[]{:S(2)}) collective-permute-start(f32[16,1024]{1,0:T(8,128)S(1)} %get-tuple-element.45), channel_id=1, source_target_pairs={{0,32},{4,36},{8,40},{12,44},{16,48},{20,52},{24,56},{28,60},{32,0... | collective-permute-start | bytes 196616 | tf_op jit(solution)/shard_map/ppermute | solution.py:329
  27.0 5.9 %collective-permute-start.5 = (f32[16,1024]{1,0:T(8,128)S(1)}, f32[16,1024]{1,0:T(8,128)S(1)}, u32[]{:S(2)}, u32[]{:S(2)}) collective-permute-start(f32[16,1024]{1,0:T(8,128)S(1)} %get-tuple-element.47), channel_id=1, source_target_pairs={{0,64},{4,68},{8,72},{12,76},{16,80},{20,84},{24,88},{28,92},{32,9... | collective-permute-start | bytes 196616 | tf_op jit(solution)/shard_map/ppermute | solution.py:329
  32.9 6.8 %collective-permute-start.6 = (f32[16,1024]{1,0:T(8,128)S(1)}, f32[16,1024]{1,0:T(8,128)S(1)}, u32[]{:S(2)}, u32[]{:S(2)}) collective-permute-start(f32[16,1024]{1,0:T(8,128)S(1)} %get-tuple-element.50), channel_id=1, source_target_pairs={{0,224},{4,228},{8,232},{12,236},{16,240},{20,244},{24,248},{28,25... | collective-permute-start | bytes 196616 | tf_op jit(solution)/shard_map/ppermute | solution.py:329
  40.5 15.2 %collective-permute-start.11 = (bf16[256,512]{1,0:T(8,128)(2,1)S(1)}, bf16[256,512]{1,0:T(8,128)(2,1)S(1)}, u32[]{:S(2)}, u32[]{:S(2)}) collective-permute-start(bf16[256,512]{1,0:T(8,128)(2,1)S(1)} %gate.3.refs_0_), channel_id=1, source_target_pairs={{0,2},{1,3},{2,0},{3,1},{4,6},{5,7},{6,4},{7,5},{8,10},{9,11},{10,... | collective-permute-start | bytes 786440 | tf_op jit(solution)/shard_map/ppermute | solution.py:310
  41.6 14.6 %collective-permute-start.8 = (bf16[256,512]{1,0:T(8,128)(2,1)S(1)}, bf16[256,512]{1,0:T(8,128)(2,1)S(1)}, u32[]{:S(2)}, u32[]{:S(2)}) collective-permute-start(bf16[256,512]{1,0:T(8,128)(2,1)S(1)} %gate.2.refs_0_), channel_id=1, source_target_pairs={{0,2},{1,3},{2,0},{3,1},{4,6},{5,7},{6,4},{7,5},{8,10},{9,11},{10,... | collective-permute-start | bytes 786440 | tf_op jit(solution)/shard_map/ppermute | solution.py:310
  43.0 14.8 %collective-permute-start.10 = (bf16[256,512]{1,0:T(8,128)(2,1)S(1)}, bf16[256,512]{1,0:T(8,128)(2,1)S(1)}, u32[]{:S(2)}, u32[]{:S(2)}) collective-permute-start(bf16[256,512]{1,0:T(8,128)(2,1)S(1)} %gate.3.refs_0_), channel_id=1, source_target_pairs={{0,1},{1,0},{2,3},{3,2},{4,5},{5,4},{6,7},{7,6},{8,9},{9,8},{10,11... | collective-permute-start | bytes 786440 | tf_op jit(solution)/shard_map/ppermute | solution.py:311
  55.7 2.1 %collective-permute-start.12 = (bf16[256,512]{1,0:T(8,128)(2,1)S(1)}, bf16[256,512]{1,0:T(8,128)(2,1)S(1)}, u32[]{:S(2)}, u32[]{:S(2)}) collective-permute-start(bf16[256,512]{1,0:T(8,128)(2,1)S(1)} %collective-permute-done.11.refs_2_), channel_id=1, source_target_pairs={{0,1},{1,0},{2,3},{3,2},{4,5},{5,4},{6,7},{7,6},{8,9},{9,8},{10,11... | collective-permute-start | bytes 786440 | tf_op jit(solution)/shard_map/ppermute | solution.py:311
  55.8 3.3 %collective-permute-start.7 = (bf16[256,512]{1,0:T(8,128)(2,1)S(1)}, bf16[256,512]{1,0:T(8,128)(2,1)S(1)}, u32[]{:S(2)}, u32[]{:S(2)}) collective-permute-start(bf16[256,512]{1,0:T(8,128)(2,1)S(1)} %gate.2.refs_0_), channel_id=1, source_target_pairs={{0,1},{1,0},{2,3},{3,2},{4,5},{5,4},{6,7},{7,6},{8,9},{9,8},{10,11... | collective-permute-start | bytes 786440 | tf_op jit(solution)/shard_map/ppermute | solution.py:311
  56.3 2.9 %collective-permute-start.9 = (bf16[256,512]{1,0:T(8,128)(2,1)S(1)}, bf16[256,512]{1,0:T(8,128)(2,1)S(1)}, u32[]{:S(2)}, u32[]{:S(2)}) collective-permute-start(bf16[256,512]{1,0:T(8,128)(2,1)S(1)} %collective-permute-done.8.refs_2_), channel_id=1, source_target_pairs={{0,1},{1,0},{2,3},{3,2},{4,5},{5,4},{6,7},{7,6},{8,9},{9,8},{10,11... | collective-permute-start | bytes 786440 | tf_op jit(solution)/shard_map/ppermute | solution.py:311

commit v2 on v1

--- a/solution.py
+++ b/solution.py
@@ -15,7 +15,8 @@
 LOCAL_AT = 2
 LOCAL_LIMIT = 50
 INPUT_LIMIT = 52
-LOAD_LIMIT = 38
+LOAD_LIMIT = 43
+LOAD_AT = (3, 4)
 HOLD = 9
 VMEM = pl.BlockSpec(memory_space=pltpu.VMEM)
 HBM = pl.BlockSpec(memory_space=pltpu.HBM)
@@ -233,7 +234,7 @@
 
 
 def load_kernel(order_ref, w_hbm, *refs):
-    rows_refs, sems = refs[:4], refs[4]
+    rows_refs, sems = refs[:-1], refs[-1]
     depth = w_hbm.shape[0] // 4
     copies = []
     for number, rows_ref in enumerate(rows_refs):
@@ -246,14 +247,15 @@
 
 def load_rows(order, weight):
     depth, features = weight.shape[0] // 4, weight.shape[1]
+    count = order.shape[0]
     return pl.pallas_call(
         load_kernel,
-        out_shape=[jax.ShapeDtypeStruct((depth, features), weight.dtype)] * 4,
+        out_shape=[jax.ShapeDtypeStruct((depth, features), weight.dtype)] * count,
         in_specs=[SMEM, HBM],
-        out_specs=[VMEM] * 4,
-        scratch_shapes=[pltpu.SemaphoreType.DMA((4,))],
+        out_specs=[VMEM] * count,
+        scratch_shapes=[pltpu.SemaphoreType.DMA((count,))],
         compiler_params=params(LOAD_LIMIT),
-        cost_estimate=cost(0, 2 * weight.size),
+        cost_estimate=cost(0, 2 * count * depth * features),
         name="load_rows",
     )(order, weight)
 
@@ -322,28 +324,33 @@
         total = total + jnp.exp(-rates * float(block - 1 - t)) * first[t][None]
 
     before = jnp.zeros_like(total)
-    due = ()
-    for level, (size, partner) in enumerate(partners(count)):
+    due, loaded = (), []
+    levels = partners(count)
+    places = [((position & size) != 0, (block * (position & (size - 1))).astype(jnp.float32)) for size, _ in levels]
+    total, places, order = lax.optimization_barrier((total, places, order))
+    for level, (size, partner) in enumerate(levels):
         total, before, *_ = lax.optimization_barrier((total, before, *due))
         due = ()
         other = lax.ppermute(total, "ctx", list(enumerate(partner)))
         if level == LOCAL_AT:
             y, f = local_part(p, prev, taps, tables, u, tied(first, total))
             due = (y,)
-        later = (position // size) % 2 == 1
-        offset = (position % size).astype(jnp.float32)
-        decay = jnp.exp(-rates * (block * offset))
+        if level in LOAD_AT:
+            loaded += load_rows(tied(order, total)[len(loaded) : len(loaded) + 4 // len(LOAD_AT)], out_weight)
+            due += tuple(loaded[-1:])
+        later, offset = places[level]
+        decay = jnp.exp(-rates * offset)
         before = before + jnp.where(later, other * decay, 0.0)
         whole = jnp.exp(-rates * float(block * size))
         total = jnp.where(later, other * whole + total, total * whole + other)
 
-    acc, start, loaded, accs = None, 0, None, []
+    acc, start, accs = None, 0, []
     for number, width in enumerate(PARTS):
         mine = gate(start, start + width, y, f, before, tables)
-        if loaded is None:
+        if not loaded:
             loaded = load_rows(tied(order, mine), out_weight)
         across, beside = over_x(mine), over_core(mine)
-        hold = loaded[:1] if number == 0 else accs[: number - HOLD + 1][-1:] if number >= HOLD else ()
+        hold = loaded[:1] if number == 0 and not LOAD_AT else accs[: number - HOLD + 1][-1:] if number >= HOLD else ()
         far = over_core(tied(across, *hold) if hold else across)
         kind = jnp.float32 if start + width < channels else jnp.bfloat16
         acc = project((mine, beside, across, far), loaded, start, acc, kind)

time: 61.5 us -> 61.6 us (level)
  waiting for transfers between devices: 9.25 us -> 5.15 us
  starting transfers between devices: 34.3 us -> 36.9 us
  Pallas kernels: 15.4 us -> 17 us
    ppermute x4, starting transfers between devices: 10.8 us -> 15.2 us  [per_device(): lax.ppermute(value, 'chan', [(i, i ^ 1) for i in range(4)])]
    ppermute x6, waiting for transfers between devices: 9.23 us -> 5.14 us  [per_device(): other = lax.ppermute(total, 'ctx', list(enumerate(partner)))]
    ppermute x6, starting transfers between devices: 17.7 us -> 16 us  [per_device(): other = lax.ppermute(total, 'ctx', list(enumerate(partner)))]
    pallas_call x1 -> x2, Pallas kernels: 4.05 us -> 5.57 us  [load_rows(): pl.pallas_call(load_kernel, out_shape=[jax.ShapeDtypeStruct((depth, featu...]
  transfers between devices with their start and end apart: 13 -> 13, of which waited for: 5 -> 3; matrix products, arithmetic and copies ran while one was open for 0% -> 0% of each run, Pallas kernels for 21% -> 23%
where the time goes in v2:
time: 61.6 us; the launch traced here: 61.4 us
  starting transfers between devices  36.9 us (60%)
  Pallas kernels  17 us (28%)
  waiting for transfers between devices  5.15 us (8%)
  local copies, waits for them, and re-layouts  1.73 us (3%)
    ppermute x6, starting transfers between devices, per_device(): other = lax.ppermute(total, 'ctx', list(enumerate(partner)))  16 us
    ppermute x4, starting transfers between devices, per_device(): lax.ppermute(value, 'chan', [(i, i ^ 1) for i in range(4)])  15.2 us
    pallas_call x2, Pallas kernels, load_rows(): pl.pallas_call(load_kernel, out_shape=[jax.ShapeDtypeStruct((depth, featu...  5.57 us
    ppermute x6, waiting for transfers between devices, per_device(): other = lax.ppermute(total, 'ctx', list(enumerate(partner)))  5.14 us
    ppermute x1, starting transfers between devices, per_device(): lax.ppermute(p[:, block - (TAPS - 1):], 'ctx', [(i, i + 1) for i in range...  4.03 us
    pallas_call x2, Pallas kernels, project(): pl.pallas_call(functools.partial(project_kernel, first, len(extra)), out_...  3.42 us
    pallas_call x1, Pallas kernels, local_part(): pl.pallas_call(local_kernel, out_shape=(tiled, tiled), in_specs=[HBM] + [...  2.99 us
    pallas_call x1, Pallas kernels, conv_input(): pl.pallas_call(input_kernel, out_shape=(jax.ShapeDtypeStruct((block * cha...  2.06 us
  transfers between devices with their start and end apart: 13, of which 3 were waited for; matrix products, arithmetic and copies ran while one was open for 0% of the time, Pallas kernels for 23%

profile of v2, /device:TPU:1, one launch (start us, length us, event | category | flops | bytes accessed | tf_op | source)
XLA Modules:
  0.0 61.4 jit_solution(1185124934133560730)
XLA Ops:
  0.0 0.8 %slice.54 = bf16[3,2,1024]{2,1,0:T(2,128)(2,1)S(1)} slice(bf16[3,256,1024]{2,1,0:T(8,128)(2,1)} %bitcast.123), slice={[0:3], [254:256], [0:1024]} | slice | bytes 24576 | tf_op jit(solution)/shard_map/slice | solution.py:316
  0.8 4.0 %collective-permute-start = (bf16[3,2,1024]{2,1,0:T(2,128)(2,1)S(1)}, bf16[3,2,1024]{2,1,0:T(2,128)(2,1)S(1)}, u32[]{:S(2)}, u32[]{:S(2)}) collective-permute-start(bf16[3,2,1024]{2,1,0:T(2,128)(2,1)S(1)} %slice.54), channel_id=1, source_target_pairs={{0,4},{4,8},{8,12},{12,16},{16,20},{20,24},{24,28},{28,32},{32,36}... | collective-permute-start | bytes 36872 | tf_op jit(solution)/shard_map/ppermute | solution.py:316
  4.9 0.0 copy-start.2
  4.9 0.8 %copy-done.2 = f32[3,3,1024]{2,1,0:T(4,128)S(1)} copy-done((f32[3,3,1024]{2,1,0:T(4,128)S(1)}, f32[3,3,1024]{2,1,0:T(4,128)}, u32[]{:S(2)}) %copy-start.2) | copy-done | bytes 36888
  5.7 0.0 copy-start
  5.7 0.0 copy-start.1
  5.7 2.1 %conv_input.1 = (f32[2048,128]{1,0:T(8,128)S(1)}, f32[2,2,1024]{2,1,0:T(2,128)S(1)}, f32[3,3,1024]{2,1,0:T(4,128)S(1)}) custom-call(bf16[3,256,1024]{2,1,0:T(8,128)(2,1)} %bitcast.124, f32[3,3,1024]{2,1,0:T(4,128)S(1)} %copy-done.2), custom_call_target="tpu_custom_call" | custom-call | flops 8000000000 | bytes 1572864 | tf_op jit(solution)/shard_map/conv_input/pallas_call | solution.py:67
  7.8 0.1 pad_add_fusion
  7.9 0.0 copy-done
  7.9 0.0 copy-done.1
  7.9 1.4 %end_state.1 = (f32[16,1024]{1,0:T(8,128)S(1)}, f32[2,16,1024]{2,1,0:T(8,128)S(1)}) custom-call(f32[2048,128]{1,0:T(8,128)S(1)} %get-tuple-element.46.u_ref.in_ref, f32[16,1024]{1,0:T(8,128)S(1)} %bitcast.120, f32[16,1024]{1,0:T(8,128)S(1)} %bitcast.121), custom_call_target="tpu_custom_call" | custom-call | flops 8388608 | bytes 1048576 | tf_op jit(solution)/shard_map/end_state/pallas_call | solution.py:108
  9.3 0.0 collective-permute-done.prev_ref
  9.5 1.4 %collective-permute-start.1 = (f32[16,1024]{1,0:T(8,128)S(1)}, f32[16,1024]{1,0:T(8,128)S(1)}, u32[]{:S(2)}, u32[]{:S(2)}) collective-permute-start(f32[16,1024]{1,0:T(8,128)S(1)} %fusion.27), channel_id=1, source_target_pairs={{0,4},{4,0},{8,12},{12,8},{16,20},{20,16},{24,28},{28,24},{32,36},... | collective-permute-start | bytes 196616 | tf_op jit(solution)/shard_map/ppermute | solution.py:334
  10.9 1.8 %collective-permute-done.1 = f32[16,1024]{1,0:T(8,128)S(1)} collective-permute-done((f32[16,1024]{1,0:T(8,128)S(1)}, f32[16,1024]{1,0:T(8,128)S(1)}, u32[]{:S(2)}, u32[]{:S(2)}) %collective-permute-start.1) | collective-permute-done | bytes 65568 | tf_op jit(solution)/shard_map/ppermute | solution.py:334
  12.7 3.9 %collective-permute-start.2 = (f32[16,1024]{1,0:T(8,128)S(1)}, f32[16,1024]{1,0:T(8,128)S(1)}, u32[]{:S(2)}, u32[]{:S(2)}) collective-permute-start(f32[16,1024]{1,0:T(8,128)S(1)} %get-tuple-element.56), channel_id=1, source_target_pairs={{0,12},{4,8},{8,4},{12,0},{16,28},{20,24},{24,20},{28,16},{32,44},... | collective-permute-start | bytes 196616 | tf_op jit(solution)/shard_map/ppermute | solution.py:334
  16.7 1.7 %collective-permute-done.2 = f32[16,1024]{1,0:T(8,128)S(1)} collective-permute-done((f32[16,1024]{1,0:T(8,128)S(1)}, f32[16,1024]{1,0:T(8,128)S(1)}, u32[]{:S(2)}, u32[]{:S(2)}) %collective-permute-start.2) | collective-permute-done | bytes 65568 | tf_op jit(solution)/shard_map/ppermute | solution.py:334
  18.4 2.0 %collective-permute-start.3 = (f32[16,1024]{1,0:T(8,128)S(1)}, f32[16,1024]{1,0:T(8,128)S(1)}, u32[]{:S(2)}, u32[]{:S(2)}) collective-permute-start(f32[16,1024]{1,0:T(8,128)S(1)} %get-tuple-element.59), channel_id=1, source_target_pairs={{0,16},{4,20},{8,24},{12,28},{16,0},{20,4},{24,8},{28,12},{32,48},... | collective-permute-start | bytes 196616 | tf_op jit(solution)/shard_map/ppermute | solution.py:334
  20.4 3.0 %local_part.1 = (f32[2048,128]{1,0:T(8,128)S(1)}, f32[2048,128]{1,0:T(8,128)S(1)}) custom-call(bf16[3,256,1024]{2,1,0:T(8,128)(2,1)} %bitcast.125, bf16[3,2,1024]{2,1,0:T(2,128)(2,1)S(1)} %collective-permute-done.prev_ref, f32[3,3,1024]{2,1,0:T(4,128)S(1)} %get-tuple-element.45.taps_ref, f32[2,16,1024]{2,1,0:T(8,128)S(1)} %get-tuple-element.47.tables_ref, ...), custom_call_target="tpu_custom_call" | custom-call | flops 16777216 | bytes 1572864 | tf_op jit(solution)/shard_map/local_part/pallas_call | solution.py:171
  23.4 0.0 collective-permute-done.3
  23.4 1.7 %collective-permute-start.4 = (f32[16,1024]{1,0:T(8,128)S(1)}, f32[16,1024]{1,0:T(8,128)S(1)}, u32[]{:S(2)}, u32[]{:S(2)}) collective-permute-start(f32[16,1024]{1,0:T(8,128)S(1)} %get-tuple-element.68), channel_id=1, source_target_pairs={{0,32},{4,36},{8,40},{12,44},{16,48},{20,52},{24,56},{28,60},{32,0... | collective-permute-start | bytes 196616 | tf_op jit(solution)/shard_map/ppermute | solution.py:334
  25.2 2.8 %load_rows.2 = (bf16[1024,1024]{1,0:T(8,128)(2,1)S(1)}, bf16[1024,1024]{1,0:T(8,128)(2,1)S(1)}) custom-call(s32[2]{0:T(128)S(1)} %bitcast.122, bf16[4096,1024]{1,0:T(8,128)(2,1)} %w_hbm.3), custom_call_target="tpu_custom_call" | custom-call | bytes 4194304 | tf_op jit(solution)/shard_map/load_rows/pallas_call | solution.py:251
  27.9 0.0 collective-permute-done.4
  28.0 3.9 %collective-permute-start.5 = (f32[16,1024]{1,0:T(8,128)S(1)}, f32[16,1024]{1,0:T(8,128)S(1)}, u32[]{:S(2)}, u32[]{:S(2)}) collective-permute-start(f32[16,1024]{1,0:T(8,128)S(1)} %get-tuple-element.74), channel_id=1, source_target_pairs={{0,64},{4,68},{8,72},{12,76},{16,80},{20,84},{24,88},{28,92},{32,9... | collective-permute-start | bytes 196616 | tf_op jit(solution)/shard_map/ppermute | solution.py:334
  32.0 0.1 slice.53.order_ref
  32.0 2.8 %load_rows.3 = (bf16[1024,1024]{1,0:T(8,128)(2,1)S(1)}, bf16[1024,1024]{1,0:T(8,128)(2,1)S(1)}) custom-call(s32[2]{0:T(128)S(1)} %slice.53.order_ref, bf16[4096,1024]{1,0:T(8,128)(2,1)} %w_hbm.3), custom_call_target="tpu_custom_call" | custom-call | bytes 4194304 | tf_op jit(solution)/shard_map/load_rows/pallas_call | solution.py:251
  34.8 0.0 collective-permute-done.5
  34.9 3.0 %collective-permute-start.6 = (f32[16,1024]{1,0:T(8,128)S(1)}, f32[16,1024]{1,0:T(8,128)S(1)}, u32[]{:S(2)}, u32[]{:S(2)}) collective-permute-start(f32[16,1024]{1,0:T(8,128)S(1)} %get-tuple-element.81), channel_id=1, source_target_pairs={{0,224},{4,228},{8,232},{12,236},{16,240},{20,244},{24,248},{28,25... | collective-permute-start | bytes 196616 | tf_op jit(solution)/shard_map/ppermute | solution.py:334
  37.9 1.7 %collective-permute-done.6 = f32[16,1024]{1,0:T(8,128)S(1)} collective-permute-done((f32[16,1024]{1,0:T(8,128)S(1)}, f32[16,1024]{1,0:T(8,128)S(1)}, u32[]{:S(2)}, u32[]{:S(2)}) %collective-permute-start.6) | collective-permute-done | bytes 65568 | tf_op jit(solution)/shard_map/ppermute | solution.py:334
  39.6 0.8 %gate.3.refs_0_ = bf16[256,512]{1,0:T(8,128)(2,1)S(1)} custom-call(f32[2048,128]{1,0:T(8,128)S(1)} %get-tuple-element.61.y_ref, f32[2048,128]{1,0:T(8,128)S(1)} %get-tuple-element.62.f_ref, f32[16,1024]{1,0:T(8,128)S(1)} %fusion.1.state_ref, f32[2,16,1024]{2,1,0:T(8,128)S(1)} %get-tuple-element.47.tables_ref), custom_call_target="tpu_custom_call" | custom-call | flops 4194304 | bytes 786432 | tf_op jit(solution)/shard_map/gate/pallas_call | solution.py:225
  40.4 1.3 %collective-permute-start.11 = (bf16[256,512]{1,0:T(8,128)(2,1)S(1)}, bf16[256,512]{1,0:T(8,128)(2,1)S(1)}, u32[]{:S(2)}, u32[]{:S(2)}) collective-permute-start(bf16[256,512]{1,0:T(8,128)(2,1)S(1)} %gate.3.refs_0_), channel_id=1, source_target_pairs={{0,2},{1,3},{2,0},{3,1},{4,6},{5,7},{6,4},{7,5},{8,10},{9,11},{10,... | collective-permute-start | bytes 786440 | tf_op jit(solution)/shard_map/ppermute | solution.py:312
  41.7 0.8 %gate.2.refs_0_ = bf16[256,512]{1,0:T(8,128)(2,1)S(1)} custom-call(f32[2048,128]{1,0:T(8,128)S(1)} %get-tuple-element.61.y_ref, f32[2048,128]{1,0:T(8,128)S(1)} %get-tuple-element.62.f_ref, f32[16,1024]{1,0:T(8,128)S(1)} %fusion.1.state_ref, f32[2,16,1024]{2,1,0:T(8,128)S(1)} %get-tuple-element.47.tables_ref), custom_call_target="tpu_custom_call" | custom-call | flops 4194304 | bytes 786432 | tf_op jit(solution)/shard_map/gate/pallas_call | solution.py:225
  42.4 0.3 collective-permute-start.8
  42.8 8.9 %collective-permute-start.10 = (bf16[256,512]{1,0:T(8,128)(2,1)S(1)}, bf16[256,512]{1,0:T(8,128)(2,1)S(1)}, u32[]{:S(2)}, u32[]{:S(2)}) collective-permute-start(bf16[256,512]{1,0:T(8,128)(2,1)S(1)} %gate.3.refs_0_), channel_id=1, source_target_pairs={{0,1},{1,0},{2,3},{3,2},{4,5},{5,4},{6,7},{7,6},{8,9},{9,8},{10,11... | collective-permute-start | bytes 786440 | tf_op jit(solution)/shard_map/ppermute | solution.py:313
  51.7 0.0 collective-permute-done.11.refs_2_
  51.7 3.5 %collective-permute-start.12 = (bf16[256,512]{1,0:T(8,128)(2,1)S(1)}, bf16[256,512]{1,0:T(8,128)(2,1)S(1)}, u32[]{:S(2)}, u32[]{:S(2)}) collective-permute-start(bf16[256,512]{1,0:T(8,128)(2,1)S(1)} %collective-permute-done.11.refs_2_), channel_id=1, source_target_pairs={{0,1},{1,0},{2,3},{3,2},{4,5},{5,4},{6,7},{7,6},{8,9},{9,8},{10,11... | collective-permute-start | bytes 786440 | tf_op jit(solution)/shard_map/ppermute | solution.py:313
  55.1 0.0 collective-permute-start.7
  55.1 0.0 collective-permute-done.8.refs_2_
  55.1 2.8 %collective-permute-start.9 = (bf16[256,512]{1,0:T(8,128)(2,1)S(1)}, bf16[256,512]{1,0:T(8,128)(2,1)S(1)}, u32[]{:S(2)}, u32[]{:S(2)}) collective-permute-start(bf16[256,512]{1,0:T(8,128)(2,1)S(1)} %collective-permute-done.8.refs_2_), channel_id=1, source_target_pairs={{0,1},{1,0},{2,3},{3,2},{4,5},{5,4},{6,7},{7,6},{8,9},{9,8},{10,11... | collective-permute-start | bytes 786440 | tf_op jit(solution)/shard_map/ppermute | solution.py:313
  58.0 0.0 collective-permute-done.10.refs_1_
  58.0 0.0 collective-permute-done.12.refs_3_
  58.0 1.3 %project.2.refs_8_ = f32[256,1024]{1,0:T(8,128)S(1)} custom-call(bf16[256,512]{1,0:T(8,128)(2,1)S(1)} %gate.3.refs_0_, bf16[256,512]{1,0:T(8,128)(2,1)S(1)} %collective-permute-done.10.refs_1_, bf16[256,512]{1,0:T(8,128)(2,1)S(1)} %collective-permute-done.11.refs_2_, bf16[256,512]{1,0:T(8,128)(2,1)S(1)} %collective-permute-done.12.refs_3_, ...), custom_call_target="tpu_custom_call" | custom-call | bytes 1024 | tf_op jit(solution)/shard_map/project/pallas_call | solution.py:277
  59.3 0.0 collective-permute-done.7.refs_1_
  59.3 0.0 collective-permute-done.9.refs_3_
  59.3 2.1 %project.3 = bf16[256,1024]{1,0:T(8,128)(2,1)} custom-call(bf16[256,512]{1,0:T(8,128)(2,1)S(1)} %gate.2.refs_0_, bf16[256,512]{1,0:T(8,128)(2,1)S(1)} %collective-permute-done.7.refs_1_, bf16[256,512]{1,0:T(8,128)(2,1)S(1)} %collective-permute-done.8.refs_2_, bf16[256,512]{1,0:T(8,128)(2,1)S(1)} %collective-permute-done.9.refs_3_, ...), custom_call_target="tpu_custom_call" | custom-call | bytes 1024 | tf_op jit(solution)/shard_map/project/pallas_call | solution.py:277
  (16 shorter events, 0.4 us)
Async XLA Ops:
  0.8 8.5 %collective-permute-start = (bf16[3,2,1024]{2,1,0:T(2,128)(2,1)S(1)}, bf16[3,2,1024]{2,1,0:T(2,128)(2,1)S(1)}, u32[]{:S(2)}, u32[]{:S(2)}) collective-permute-start(bf16[3,2,1024]{2,1,0:T(2,128)(2,1)S(1)} %slice.54), channel_id=1, source_target_pairs={{0,4},{4,8},{8,12},{12,16},{16,20},{20,24},{24,28},{28,32},{32,36}... | collective-permute-start | bytes 36872 | tf_op jit(solution)/shard_map/ppermute | solution.py:316
  4.9 0.8 %copy-start.2 = (f32[3,3,1024]{2,1,0:T(4,128)S(1)}, f32[3,3,1024]{2,1,0:T(4,128)}, u32[]{:S(2)}) copy-start(f32[3,3,1024]{2,1,0:T(4,128)} %taps_ref.1) | copy-start | bytes 110596
  5.7 2.2 %copy-start = (f32[1024,16]{0,1:T(8,128)S(1)}, f32[1024,16]{0,1:T(8,128)}, u32[]{:S(2)}) copy-start(f32[1024,16]{0,1:T(8,128)} %param.7) | copy-start | bytes 196612
  5.7 2.2 %copy-start.1 = (f32[1024,16]{0,1:T(8,128)S(1)}, f32[1024,16]{0,1:T(8,128)}, u32[]{:S(2)}) copy-start(f32[1024,16]{0,1:T(8,128)} %param.8) | copy-start | bytes 196612
  9.5 3.2 %collective-permute-start.1 = (f32[16,1024]{1,0:T(8,128)S(1)}, f32[16,1024]{1,0:T(8,128)S(1)}, u32[]{:S(2)}, u32[]{:S(2)}) collective-permute-start(f32[16,1024]{1,0:T(8,128)S(1)} %fusion.27), channel_id=1, source_target_pairs={{0,4},{4,0},{8,12},{12,8},{16,20},{20,16},{24,28},{28,24},{32,36},... | collective-permute-start | bytes 196616 | tf_op jit(solution)/shard_map/ppermute | solution.py:334
  12.7 5.6 %collective-permute-start.2 = (f32[16,1024]{1,0:T(8,128)S(1)}, f32[16,1024]{1,0:T(8,128)S(1)}, u32[]{:S(2)}, u32[]{:S(2)}) collective-permute-start(f32[16,1024]{1,0:T(8,128)S(1)} %get-tuple-element.56), channel_id=1, source_target_pairs={{0,12},{4,8},{8,4},{12,0},{16,28},{20,24},{24,20},{28,16},{32,44},... | collective-permute-start | bytes 196616 | tf_op jit(solution)/shard_map/ppermute | solution.py:334
  18.4 5.0 %collective-permute-start.3 = (f32[16,1024]{1,0:T(8,128)S(1)}, f32[16,1024]{1,0:T(8,128)S(1)}, u32[]{:S(2)}, u32[]{:S(2)}) collective-permute-start(f32[16,1024]{1,0:T(8,128)S(1)} %get-tuple-element.59), channel_id=1, source_target_pairs={{0,16},{4,20},{8,24},{12,28},{16,0},{20,4},{24,8},{28,12},{32,48},... | collective-permute-start | bytes 196616 | tf_op jit(solution)/shard_map/ppermute | solution.py:334
  23.4 4.5 %collective-permute-start.4 = (f32[16,1024]{1,0:T(8,128)S(1)}, f32[16,1024]{1,0:T(8,128)S(1)}, u32[]{:S(2)}, u32[]{:S(2)}) collective-permute-start(f32[16,1024]{1,0:T(8,128)S(1)} %get-tuple-element.68), channel_id=1, source_target_pairs={{0,32},{4,36},{8,40},{12,44},{16,48},{20,52},{24,56},{28,60},{32,0... | collective-permute-start | bytes 196616 | tf_op jit(solution)/shard_map/ppermute | solution.py:334
  28.0 6.8 %collective-permute-start.5 = (f32[16,1024]{1,0:T(8,128)S(1)}, f32[16,1024]{1,0:T(8,128)S(1)}, u32[]{:S(2)}, u32[]{:S(2)}) collective-permute-start(f32[16,1024]{1,0:T(8,128)S(1)} %get-tuple-element.74), channel_id=1, source_target_pairs={{0,64},{4,68},{8,72},{12,76},{16,80},{20,84},{24,88},{28,92},{32,9... | collective-permute-start | bytes 196616 | tf_op jit(solution)/shard_map/ppermute | solution.py:334
  34.9 4.7 %collective-permute-start.6 = (f32[16,1024]{1,0:T(8,128)S(1)}, f32[16,1024]{1,0:T(8,128)S(1)}, u32[]{:S(2)}, u32[]{:S(2)}) collective-permute-start(f32[16,1024]{1,0:T(8,128)S(1)} %get-tuple-element.81), channel_id=1, source_target_pairs={{0,224},{4,228},{8,232},{12,236},{16,240},{20,244},{24,248},{28,25... | collective-permute-start | bytes 196616 | tf_op jit(solution)/shard_map/ppermute | solution.py:334
  40.4 11.3 %collective-permute-start.11 = (bf16[256,512]{1,0:T(8,128)(2,1)S(1)}, bf16[256,512]{1,0:T(8,128)(2,1)S(1)}, u32[]{:S(2)}, u32[]{:S(2)}) collective-permute-start(bf16[256,512]{1,0:T(8,128)(2,1)S(1)} %gate.3.refs_0_), channel_id=1, source_target_pairs={{0,2},{1,3},{2,0},{3,1},{4,6},{5,7},{6,4},{7,5},{8,10},{9,11},{10,... | collective-permute-start | bytes 786440 | tf_op jit(solution)/shard_map/ppermute | solution.py:312
  42.4 12.7 %collective-permute-start.8 = (bf16[256,512]{1,0:T(8,128)(2,1)S(1)}, bf16[256,512]{1,0:T(8,128)(2,1)S(1)}, u32[]{:S(2)}, u32[]{:S(2)}) collective-permute-start(bf16[256,512]{1,0:T(8,128)(2,1)S(1)} %gate.2.refs_0_), channel_id=1, source_target_pairs={{0,2},{1,3},{2,0},{3,1},{4,6},{5,7},{6,4},{7,5},{8,10},{9,11},{10,... | collective-permute-start | bytes 786440 | tf_op jit(solution)/shard_map/ppermute | solution.py:312
  42.8 15.2 %collective-permute-start.10 = (bf16[256,512]{1,0:T(8,128)(2,1)S(1)}, bf16[256,512]{1,0:T(8,128)(2,1)S(1)}, u32[]{:S(2)}, u32[]{:S(2)}) collective-permute-start(bf16[256,512]{1,0:T(8,128)(2,1)S(1)} %gate.3.refs_0_), channel_id=1, source_target_pairs={{0,1},{1,0},{2,3},{3,2},{4,5},{5,4},{6,7},{7,6},{8,9},{9,8},{10,11... | collective-permute-start | bytes 786440 | tf_op jit(solution)/shard_map/ppermute | solution.py:313
  51.7 6.3 %collective-permute-start.12 = (bf16[256,512]{1,0:T(8,128)(2,1)S(1)}, bf16[256,512]{1,0:T(8,128)(2,1)S(1)}, u32[]{:S(2)}, u32[]{:S(2)}) collective-permute-start(bf16[256,512]{1,0:T(8,128)(2,1)S(1)} %collective-permute-done.11.refs_2_), channel_id=1, source_target_pairs={{0,1},{1,0},{2,3},{3,2},{4,5},{5,4},{6,7},{7,6},{8,9},{9,8},{10,11... | collective-permute-start | bytes 786440 | tf_op jit(solution)/shard_map/ppermute | solution.py:313
  55.1 4.1 %collective-permute-start.7 = (bf16[256,512]{1,0:T(8,128)(2,1)S(1)}, bf16[256,512]{1,0:T(8,128)(2,1)S(1)}, u32[]{:S(2)}, u32[]{:S(2)}) collective-permute-start(bf16[256,512]{1,0:T(8,128)(2,1)S(1)} %gate.2.refs_0_), channel_id=1, source_target_pairs={{0,1},{1,0},{2,3},{3,2},{4,5},{5,4},{6,7},{7,6},{8,9},{9,8},{10,11... | collective-permute-start | bytes 786440 | tf_op jit(solution)/shard_map/ppermute | solution.py:313
  55.1 4.1 %collective-permute-start.9 = (bf16[256,512]{1,0:T(8,128)(2,1)S(1)}, bf16[256,512]{1,0:T(8,128)(2,1)S(1)}, u32[]{:S(2)}, u32[]{:S(2)}) collective-permute-start(bf16[256,512]{1,0:T(8,128)(2,1)S(1)} %collective-permute-done.8.refs_2_), channel_id=1, source_target_pairs={{0,1},{1,0},{2,3},{3,2},{4,5},{5,4},{6,7},{7,6},{8,9},{9,8},{10,11... | collective-permute-start | bytes 786440 | tf_op jit(solution)/shard_map/ppermute | solution.py:313
